TPU v7x, 512 devices: a whole 4x8x8 slice. The times are simulated.
512 devices in a mesh: rep: 8 (over y), ep: 64 (over x, z, core).
Axes of the slice: x: 4, y: 8, z: 8, core: 2. Of those that a mesh axis runs over, the one named last changes fastest.
Arguments:
- master: float32 [3, 2048, 16384], P(None, ('rep', 'ep')), may hold values from -0.125 to 0.125
- moment_one: float32 [3, 2048, 16384], P(None, ('rep', 'ep')), may hold values from -0.02 to 0.02
- moment_two: float32 [3, 2048, 16384], P(None, ('rep', 'ep')), may hold values from 1e-05 to 0.0001
- gradient: bfloat16 [3, 2048, 16384], P(None, ('rep', 'ep')), may hold values from -0.079589844 to 0.079589844
- states: bfloat16 [2048, 2048], P(('rep', 'ep')), may hold values from -6 to 6
- norm_gain: float32 [2048], replicated, may hold values from 0.5 to 1.5
- routes: int32 [2048, 8], P(('rep', 'ep')), may hold values from 0 to 15, all different within a row; in each aligned block of 4 rows (0 to 3, 4 to 7, ...) at most 3 rows name the same one
- route_weights: float32 [2048, 8], P(('rep', 'ep')), may hold values from 0.05 to 1
Outputs:
- master_next: float32 [3, 2048, 16384], P(None, ('rep', 'ep'))
- mixture: bfloat16 [2048, 2048], P(('rep', 'ep'))
Inputs may be any that keep to these rules, and one draw needn't show every extreme that they name: `routes`: each row names 8 distinct experts. Within the 4 rows of one device no expert is named more than 3 times, and in some device's rows some expert is named exactly 3 times.
All inputs are finite; a program needn't handle non-finite values.
Results may differ from a plain program's by a relative error of at most 0.01005.
Values may be sent and summed in bfloat16 or wider, within the bound.
No kernel may reach another device: no remote copies, remote signals or barrier semaphores. Data moves between devices by JAX's collectives and lax.ppermute only.
A program may use at most 128 MiB of HBM per device.

v0:
```python
import jax
import jax.numpy as jnp
from jax import lax
from jax.sharding import PartitionSpec as P

E = 16
TOP = 8
QBLOCK = 128
STEP = 10
CAP = 3


BETA_ONE = 0.9
BETA_TWO = 0.95
LEARN_RATE = 0.01
ADAM_EPSILON = 1e-08
WEIGHT_DECAY = 0.1
SATURATION = 448.0
SCALE_EPSILON = 1e-06
NORM_EPSILON = 1e-06
SUBNORMAL_EDGE = 0.015625
MANTISSA_BITS = 3.0


def adam_update(master, moment_one, moment_two, gradient):
    grad_float = gradient.astype(jnp.float32)
    first = BETA_ONE * moment_one + (1.0 - BETA_ONE) * grad_float
    second = BETA_TWO * moment_two + (1.0 - BETA_TWO) * grad_float * grad_float
    correct_one = 1.0 - BETA_ONE**STEP
    correct_two = 1.0 - BETA_TWO**STEP
    direction = first / correct_one / (jnp.sqrt(second / correct_two) + ADAM_EPSILON)
    return master - LEARN_RATE * (direction + WEIGHT_DECAY * master)


def block_max(weights, block_size):
    stacked = weights.shape[0]
    columns = weights.shape[2]
    magnitude = jnp.abs(weights).reshape(
        stacked, weights.shape[1], columns // block_size, block_size
    )
    return jnp.max(magnitude, axis=(1, 3))


def column_scale(largest, block_size):
    return jnp.repeat((largest + SCALE_EPSILON) / SATURATION, block_size, axis=1)


def minifloat_grid(values):
    magnitude = jnp.abs(values)
    exponent = jnp.floor(jnp.log2(jnp.maximum(magnitude, SUBNORMAL_EDGE)))
    spacing = jnp.exp2(exponent - MANTISSA_BITS)
    snapped = jnp.floor(magnitude / spacing + 0.5) * spacing
    return jnp.sign(values) * snapped


def quantize(weights, scales):
    clipped = jnp.clip(weights / scales[:, None, :], -SATURATION, SATURATION)
    return minifloat_grid(clipped).astype(jnp.bfloat16)


def rms_norm(states, norm_gain):
    values = states.astype(jnp.float32)
    mean_square = jnp.mean(values * values, axis=1, keepdims=True)
    return (values * lax.rsqrt(mean_square + NORM_EPSILON) * norm_gain[None, :]).astype(
        jnp.bfloat16
    )


def body(master, moment_one, moment_two, gradient, states, norm_gain, routes, route_weights):
    updated = adam_update(master, moment_one, moment_two, gradient)
    columns = lax.all_to_all(updated, "ep", split_axis=2, concat_axis=1, tiled=True)
    largest = lax.pmax(block_max(columns, QBLOCK), "rep")
    scales = column_scale(largest, QBLOCK)
    packed = quantize(columns, scales)
    payload = lax.all_gather(packed, "rep", axis=1, tiled=True)
    normed = rms_norm(states, norm_gain)
    weights = route_weights / jnp.sum(route_weights, axis=1, keepdims=True)
    row_count = routes.shape[0]
    group_size = lax.axis_size("ep") // E
    expert_ids = routes.reshape(-1)
    onehot = (expert_ids[:, None] == jnp.arange(E, dtype=jnp.int32)[None, :]).astype(jnp.int32)
    earlier = jnp.cumsum(onehot, axis=0) - onehot
    slot_index = jnp.sum(earlier * onehot, axis=1)
    position = expert_ids * CAP + slot_index
    placed = (position[:, None] == jnp.arange(E * CAP, dtype=jnp.int32)[None, :]).astype(
        jnp.float32
    )
    placed = placed.reshape(row_count, TOP, E * CAP)
    select = jnp.sum(placed, axis=1).astype(jnp.bfloat16)
    weighted = jnp.sum(placed * weights[:, :, None], axis=1)
    gathered = lax.dot_general(
        select, normed, (((0,), (0,)), ((), ())), preferred_element_type=jnp.float32
    )
    gathered = gathered.astype(jnp.bfloat16).reshape(E, CAP, normed.shape[1])
    buffer = jnp.repeat(gathered, group_size, axis=0)
    received = lax.all_to_all(buffer, "ep", split_axis=0, concat_axis=0, tiled=True)
    sources, slot_count, model_width = received.shape
    token_rows = received.reshape(sources * slot_count, model_width)
    gate_act = (
        jnp.dot(token_rows, payload[0], preferred_element_type=jnp.float32) * scales[0][None, :]
    )
    up_act = (
        jnp.dot(token_rows, payload[1], preferred_element_type=jnp.float32) * scales[1][None, :]
    )
    hidden = (jax.nn.silu(gate_act) * up_act * scales[2][None, :]).astype(jnp.bfloat16)
    partial_value = lax.dot_general(
        hidden, payload[2], (((1,), (1,)), ((), ())), preferred_element_type=jnp.float32
    )
    partial_value = partial_value.astype(jnp.bfloat16).reshape(sources, slot_count, model_width)
    returned = lax.all_to_all(partial_value, "ep", split_axis=0, concat_axis=0, tiled=True)
    model_width = normed.shape[1]
    expert_out = jnp.sum(
        returned.astype(jnp.float32).reshape(E, group_size, CAP, model_width), axis=1
    )
    expert_out = expert_out.reshape(E * CAP, model_width)
    mixture = jnp.dot(
        weighted, expert_out, precision=lax.Precision.HIGHEST, preferred_element_type=jnp.float32
    )
    return (updated, mixture.astype(jnp.bfloat16))


def solution(mesh):
    return jax.shard_map(
        body,
        mesh=mesh,
        in_specs=(
            P(None, ("rep", "ep"), None),
            P(None, ("rep", "ep"), None),
            P(None, ("rep", "ep"), None),
            P(None, ("rep", "ep"), None),
            P(("rep", "ep"), None),
            P(),
            P(("rep", "ep"), None),
            P(("rep", "ep"), None),
        ),
        out_specs=(P(None, ("rep", "ep"), None), P(("rep", "ep"), None)),
        check_vma=False,
    )
```

profile of v0, /device:TPU:1, one launch (start us, length us, event | category | flops | bytes accessed | tf_op | source)
XLA Modules:
  0.0 262.0 jit_solution(9473306524994634455)
XLA Ops:
  7.2 3.0 %multiply_subtract_fusion = f32[3,4,16384]{2,1,0:T(4,128)S(1)} fusion(f32[3,4,16384]{2,1,0:T(4,128)} %param.8, f32[3,4,16384]{2,1,0:T(4,128)} %param.10, bf16[3,4,16384]{2,1,0:T(4,128)(2,1)} %param.11, f32[3,4,16384]{2,1,0:T(4,128)} %param.9), kind=kLoop, calls=%fused_computation.23 | loop fusion | flops 3145728 | bytes 3538944 | tf_op jit(solution)/shard_map/sub | solution.py:32
  10.2 20.3 %copy.39 = f32[3,4,16384]{1,0,2:T(4,128)} copy(f32[3,4,16384]{2,1,0:T(4,128)S(1)} %multiply_subtract_fusion) | data formatting | bytes 1572864 | tf_op jit(solution)/shard_map/sub | solution.py:32
  30.5 31.5 %reshape.81 = f32[64,1,3072]{2,1,0:T(1,128)S(1)} reshape(f32[16384,3,4]{2,1,0:T(4,128)} %bitcast.42) | data formatting | bytes 1572864
  62.0 37.6 %all_to_all.28 = f32[64,1,3072]{2,1,0:T(1,128)S(1)} all-to-all(f32[64,1,3072]{2,1,0:T(1,128)S(1)} %reshape.81), channel_id=1, replica_groups=mesh['rep'=8,'ep'=64] {'ep'}, dimensions={0} | all-to-all | bytes 1572864 | tf_op jit(solution)/shard_map/all_to_all | solution.py:71
  99.6 0.5 broadcast.77
  100.1 2.5 reduce.2
  102.6 22.4 %reshape.82 = f32[16384,3,4]{2,1,0:T(4,128)} reshape(f32[64,3072]{1,0:T(8,128)S(1)} %reduce.2) | data formatting | bytes 1572864
  125.0 22.8 %copy.40 = f32[3,4,64,256]{3,1,2,0:T(4,128)S(1)} copy(f32[3,4,64,256]{1,0,3,2:T(4,128)} %bitcast.41) | data formatting | bytes 1572864 | tf_op jit(solution)/shard_map/all_to_all | solution.py:71
  147.9 0.2 abs_reduce_fusion
  148.2 14.2 %pmax.7 = f32[3,2]{1,0:T(4,128)S(1)} all-reduce(f32[3,2]{1,0:T(4,128)S(1)} %reduce_max.18), channel_id=1, replica_groups=mesh['rep'=8,'ep'=64] {'rep'}, use_global_device_ids=true, to_apply=%region_8.9 | all-reduce | flops 6 | bytes 48 | tf_op jit(solution)/shard_map/pmax | solution.py:72
  162.5 0.3 all_to_all.23
  162.7 1.4 multiply_convert_fusion
  165.1 0.3 convolution_convert_fusion.1
  165.5 0.5 broadcast_in_dim.25
  166.0 38.0 %all_to_all.29 = bf16[64,3,2048]{2,1,0:T(4,128)(2,1)S(1)} all-to-all(bf16[64,3,2048]{2,1,0:T(4,128)(2,1)S(1)} %bitcast.44), channel_id=1, replica_groups=mesh['rep'=8,'ep'=64] {'ep'}, dimensions={0} | all-to-all | bytes 1572864 | tf_op jit(solution)/shard_map/all_to_all | solution.py:96
  204.0 0.7 reshape.74
  204.9 3.8 %all-gather.2.cloned.1.call-done = bf16[3,2048,256]{2,1,0:T(8,128)(2,1)} async-done(((bf16[3,256,256]{2,1,0:T(8,128)(2,1)}), bf16[3,2048,256]{2,1,0:T(8,128)(2,1)}) %all-gather.2.cloned.1.call-update) | async-done | bytes 3145744 | tf_op jit(solution)/shard_map/all_gather | solution.py:75
  208.7 1.6 convolution_multiply_fusion.1
  210.3 2.7 %convolution_convert_fusion = bf16[192,2048]{1,0:T(8,128)(2,1)S(1)} fusion(bf16[192,2048]{1,0:T(8,128)(2,1)S(1)} %reshape.74, bf16[3,2048,256]{2,1,0:T(8,128)(2,1)} %all-gather.2.cloned.1.call-done, f32[192,256]{1,0:T(8,128)S(1)} %convolution_multiply_fusion.1, f32[256]{0:T(256)S(1)} %get-tuple-element.11, f32[256]{0:T(256)S(1)} %get-tuple-element.12), kind=kOutput, calls=%fused_computation | convolution fusion | flops 403439616 | bytes 3868672 | tf_op jit(solution)/shard_map/dot_general | solution.py:106
  212.9 0.5 reshape.75
  213.5 40.0 %all_to_all.30 = bf16[64,3,2048]{2,1,0:T(4,128)(2,1)S(1)} all-to-all(bf16[64,3,2048]{2,1,0:T(4,128)(2,1)S(1)} %reshape.75), channel_id=1, replica_groups=mesh['rep'=8,'ep'=64] {'ep'}, dimensions={0} | all-to-all | bytes 1572864 | tf_op jit(solution)/shard_map/all_to_all | solution.py:110
  253.5 0.6 convert_reduce_fusion
  254.1 0.2 reshape.78
  254.3 0.9 convolution_convert_fusion.2
  (32 shorter events, 1.5 us)
Async XLA Ops:
  7.2 201.5 %all-gather.2.cloned.1.call-start = ((), (), s32[]{:S(2)}) async-start(), calls=%async_computation.3 | async-start | bytes 3538944 | tf_op jit(solution)/shard_map/all_gather | solution.py:75
  10.2 20.3 %copy-start = (f32[3,4,16384]{2,1,0:T(4,128)}, f32[3,4,16384]{2,1,0:T(4,128)S(1)}, u32[]{:S(2)}) copy-start(f32[3,4,16384]{2,1,0:T(4,128)S(1)} %multiply_subtract_fusion) | copy-start | bytes 2359300
  147.8 16.3 %copy-start.3 = (s32[4,8]{1,0:T(4,128)S(1)}, s32[4,8]{1,0:T(4,128)}, u32[]{:S(2)}) copy-start(s32[4,8]{1,0:T(4,128)} %param.14) | copy-start | bytes 388
  147.9 16.8 %copy-start.4 = (f32[4,8]{1,0:T(4,128)S(1)}, f32[4,8]{1,0:T(4,128)}, u32[]{:S(2)}) copy-start(f32[4,8]{1,0:T(4,128)} %param.15) | copy-start | bytes 388
  147.9 16.9 %copy-start.1 = (bf16[4,2048]{1,0:T(4,128)(2,1)S(1)}, bf16[4,2048]{1,0:T(4,128)(2,1)}, u32[]{:S(2)}) copy-start(bf16[4,2048]{1,0:T(4,128)(2,1)} %param.12) | copy-start | bytes 49156
  147.9 17.2 %copy-start.2 = (f32[2048]{0:T(1024)S(1)}, f32[2048]{0:T(1024)}, u32[]{:S(2)}) copy-start(f32[2048]{0:T(1024)} %param.13) | copy-start | bytes 24580
Sparse Core Ops, SparseCore 0:
  164.3 44.3 all-gather.1
where the time goes:
time: 263 us; the launch traced here: 262 us
  blocking collectives  130 us (49%)
  local copies, waits for them, and re-layouts  100 us (38%)
  between operations  14.2 us (5%)
  other arithmetic  8.51 us (3%)
  matrix products  5.43 us (2%)
  waiting for transfers between devices  3.83 us (1%)
    unnamed x14, local copies, waits for them, and re-layouts  53.9 us
    all_to_all x1, blocking collectives, body(): lax.all_to_all(partial_value, 'ep', split_axis=0, concat_axis=0, tiled=True)  40 us
    all_to_all x1, blocking collectives, body(): lax.all_to_all(buffer, 'ep', split_axis=0, concat_axis=0, tiled=True)  38 us
    all_to_all x1, blocking collectives, body(): lax.all_to_all(updated, 'ep', split_axis=2, concat_axis=1, tiled=True)  37.6 us
    all_to_all x3, local copies, waits for them, and re-layouts, body(): lax.all_to_all(updated, 'ep', split_axis=2, concat_axis=1, tiled=True)  23.6 us
    sub x1, local copies, waits for them, and re-layouts, adam_update(): return master - LEARN_RATE * (direction + WEIGHT_DECAY * master)  20.3 us
    pmax x1, blocking collectives, body(): largest = lax.pmax(block_max(columns, QBLOCK), 'rep')  14.2 us
  transfers between devices with their start and end apart: 1, of which 1 were waited for; matrix products, arithmetic and copies ran while one was open for 1% of the time, Pallas kernels for 0%

commit v1 on v0

v1 whole, which is shorter than its diff:
```python
import jax
import jax.numpy as jnp
from jax import lax
from jax.experimental import pallas as pl
from jax.experimental.pallas import tpu as pltpu
from jax.sharding import Mesh, PartitionSpec as P

E = 16
TOP = 8
QBLOCK = 128
STEP = 10
CAP = 3

BETA_ONE = 0.9
BETA_TWO = 0.95
LEARN_RATE = 0.01
ADAM_EPSILON = 1e-08
WEIGHT_DECAY = 0.1
SATURATION = 448.0
SCALE_EPSILON = 1e-06
NORM_EPSILON = 1e-06
SUBNORMAL_EDGE = 0.015625

BOUND = 0.1875
LEVELS = 32767.0
UNIT = BOUND / LEVELS**5

AXES = ("y", "x", "z", "c")
OWNERS = ("y", "z")
COPIES = ("x", "c")


def adam_update(master, moment_one, moment_two, gradient):
    grad_float = gradient.astype(jnp.float32)
    first = BETA_ONE * moment_one + (1.0 - BETA_ONE) * grad_float
    second = BETA_TWO * moment_two + (1.0 - BETA_TWO) * grad_float * grad_float
    correct_one = 1.0 - BETA_ONE**STEP
    correct_two = 1.0 - BETA_TWO**STEP
    direction = first / correct_one / (jnp.sqrt(second / correct_two) + ADAM_EPSILON)
    return master - LEARN_RATE * (direction + WEIGHT_DECAY * master)


def encode(weights):
    magnitude = jnp.abs(weights) * (1.0 / BOUND)
    level = jnp.floor(jnp.exp2(jnp.log2(magnitude) * 0.2) * LEVELS + 0.5)
    level = jnp.where(magnitude > 0, jnp.minimum(level, LEVELS), 0.0)
    return jnp.where(weights < 0, -level, level).astype(jnp.int32).astype(jnp.int16)


def rms_norm(states, norm_gain):
    values = states.astype(jnp.float32)
    mean_square = jnp.mean(values * values, axis=1, keepdims=True)
    return (values * lax.rsqrt(mean_square + NORM_EPSILON) * norm_gain[None, :]).astype(
        jnp.bfloat16
    )


def snap(q):
    scaled = q * 1048577.0
    normal = scaled - (scaled - q)
    small = (q + 24576.0) - 24576.0
    return jnp.where(jnp.abs(q) < SUBNORMAL_EDGE, small, normal)


def expert_kernel(codes, tokens, out, packed):
    copies, sources = codes.shape[0], codes.shape[1]
    xs = copies // 2
    groups = sources // 8

    def extremes(step, carry):
        high, low = carry
        p = step // groups
        y = step % groups
        block = codes[p, pl.ds(y * 8, 8)].astype(jnp.int32)
        return jnp.maximum(high, jnp.max(block, axis=0)), jnp.minimum(low, jnp.min(block, axis=0))

    zero = jnp.zeros((3, 8, 128), jnp.int32)
    high, low = lax.fori_loop(0, copies * groups, extremes, (zero, zero))
    top = jnp.maximum(high, -low).astype(jnp.float32)
    sub = lax.broadcasted_iota(jnp.int32, (8, 128), 0)
    scales = []
    factors = []
    for m in range(3):
        pair = []
        for h in range(2):
            level = jnp.max(
                jnp.max(top[m, 4 * h : 4 * h + 4], axis=0, keepdims=True), axis=1, keepdims=True
            )
            square = level * level
            largest = square * square * level * UNIT
            pair.append((largest + SCALE_EPSILON) / SATURATION)
        scales.append(
            jnp.concatenate([jnp.broadcast_to(v, (1, 128)) for v in pair], axis=1)
        )
        factors.append(
            jnp.where(
                sub < 4,
                jnp.broadcast_to(UNIT / pair[0], (8, 128)),
                jnp.broadcast_to(UNIT / pair[1], (8, 128)),
            )
        )

    def quantize(m):
        factor = factors[m][None]

        def values(p, y):
            level = codes[p, pl.ds(y * 8, 8), m].astype(jnp.int32).astype(jnp.float32)
            square = level * level
            q = square * square * level * factor
            return snap(jnp.clip(q, -SATURATION, SATURATION))

        def step(t, carry):
            y = t // xs
            x = t % xs
            even = values(2 * x, y)
            odd = values(2 * x + 1, y)
            first_half = (lax.broadcasted_iota(jnp.int32, even.shape, 1)) < 4
            left = jnp.where(first_half, even, pltpu.roll(odd, 4, 1))
            right = jnp.where(first_half, pltpu.roll(even, 4, 1), odd)
            rows = pl.ds(pl.multiple_of(t * 64, 64), 64)
            packed[m, rows, 0:128] = left.reshape(64, 128).astype(jnp.bfloat16)
            packed[m, rows, 128:256] = right.reshape(64, 128).astype(jnp.bfloat16)
            return carry

        lax.fori_loop(0, xs * groups, step, 0)

    for m in range(3):
        quantize(m)
    token_rows = tokens[...]
    gate_act = jnp.dot(token_rows, packed[0], preferred_element_type=jnp.float32) * scales[0]
    up_act = jnp.dot(token_rows, packed[1], preferred_element_type=jnp.float32) * scales[1]
    hidden = gate_act / (1.0 + jnp.exp(-gate_act)) * up_act * scales[2]
    out[...] = lax.dot_general(
        hidden.astype(jnp.bfloat16),
        packed[2],
        (((1,), (1,)), ((), ())),
        preferred_element_type=jnp.float32,
    ).astype(jnp.bfloat16)


def experts(codes, tokens):
    width = tokens.shape[1]
    return pl.pallas_call(
        expert_kernel,
        out_shape=jax.ShapeDtypeStruct(tokens.shape, jnp.bfloat16),
        in_specs=[pl.BlockSpec(memory_space=pltpu.VMEM)] * 2,
        out_specs=pl.BlockSpec(memory_space=pltpu.VMEM),
        scratch_shapes=[pltpu.VMEM((3, width, 256), jnp.bfloat16)],
        compiler_params=pltpu.CompilerParams(vmem_limit_bytes=40 * 2**20),
    )(codes, tokens)


def body(master, moment_one, moment_two, gradient, states, norm_gain, routes, route_weights):
    owners = lax.axis_size(OWNERS)
    updated = adam_update(master, moment_one, moment_two, gradient)
    codes = encode(updated)
    codes = codes.reshape(3, 4, owners, 2, 128).transpose(2, 0, 3, 1, 4).reshape(owners, 3, 8, 128)
    columns = lax.all_to_all(codes, OWNERS, split_axis=0, concat_axis=0, tiled=True)
    gathered_codes = lax.all_gather(columns, COPIES, axis=0, tiled=False)

    normed = rms_norm(states, norm_gain)
    weights = route_weights / jnp.sum(route_weights, axis=1, keepdims=True)
    row_count = routes.shape[0]
    group_size = owners // E
    expert_ids = routes.reshape(-1)
    onehot = (expert_ids[:, None] == jnp.arange(E, dtype=jnp.int32)[None, :]).astype(jnp.int32)
    earlier = jnp.cumsum(onehot, axis=0) - onehot
    slot_index = jnp.sum(earlier * onehot, axis=1)
    position = expert_ids * CAP + slot_index
    placed = (position[:, None] == jnp.arange(E * CAP, dtype=jnp.int32)[None, :]).astype(
        jnp.float32
    )
    placed = placed.reshape(row_count, TOP, E * CAP)
    select = jnp.sum(placed, axis=1).astype(jnp.bfloat16)
    weighted = jnp.sum(placed * weights[:, :, None], axis=1)
    gathered = lax.dot_general(
        select, normed, (((0,), (0,)), ((), ())), preferred_element_type=jnp.float32
    )
    width = normed.shape[1]
    gathered = gathered.astype(jnp.bfloat16).reshape(E, CAP, width)
    buffer = jnp.repeat(gathered, group_size, axis=0)
    received = lax.all_to_all(buffer, OWNERS, split_axis=0, concat_axis=0, tiled=True)
    tokens = received.reshape(owners * CAP, width)

    partial_value = experts(gathered_codes, tokens).reshape(owners, CAP, width)
    returned = lax.all_to_all(partial_value, OWNERS, split_axis=0, concat_axis=0, tiled=True)
    expert_out = jnp.sum(
        returned.astype(jnp.float32).reshape(E, group_size, CAP, width), axis=1
    )
    expert_out = expert_out.reshape(E * CAP, width)
    mixture = jnp.dot(
        weighted, expert_out, precision=lax.Precision.HIGHEST, preferred_element_type=jnp.float32
    )
    return (updated, mixture.astype(jnp.bfloat16))


def solution(mesh):
    chips = Mesh(mesh.devices.reshape(8, 4, 8, 2), AXES)
    rows = P(None, AXES, None)
    return jax.shard_map(
        body,
        mesh=chips,
        in_specs=(rows, rows, rows, rows, P(AXES, None), P(), P(AXES, None), P(AXES, None)),
        out_specs=(rows, P(AXES, None)),
        check_vma=False,
    )
```

time: 263 us -> 130 us (0.49)
  the two profiles are of different devices: /device:TPU:1 before, /device:TPU:20 now
where the time goes in v1:
time: 130 us
  blocking collectives  52.8 us (41%)
  waiting for transfers between devices  27.3 us (21%)
  starting transfers between devices  22.3 us (17%)
  local copies, waits for them, and re-layouts  11.4 us (9%)
  Pallas kernels  7.83 us (6%)
  other arithmetic  6.16 us (5%)
    all_to_all x1, blocking collectives, body(): lax.all_to_all(partial_value, OWNERS, split_axis=0, concat_axis=0, tiled=...  35.6 us
    all_gather x1, blocking collectives, body(): gathered_codes = lax.all_gather(columns, COPIES, axis=0, tiled=False)  17.3 us
    all_to_all x1, starting transfers between devices, body(): lax.all_to_all(codes, OWNERS, split_axis=0, concat_axis=0, tiled=True)  16.5 us
    all_to_all x1, waiting for transfers between devices, body(): lax.all_to_all(codes, OWNERS, split_axis=0, concat_axis=0, tiled=True)  15.3 us
    all_to_all x1, waiting for transfers between devices, body(): lax.all_to_all(buffer, OWNERS, split_axis=0, concat_axis=0, tiled=True)  12 us
    pallas_call x1, Pallas kernels, experts(): pl.pallas_call(expert_kernel, out_shape=jax.ShapeDtypeStruct(tokens.shape...  7.83 us
    all_to_all x1, starting transfers between devices, body(): lax.all_to_all(buffer, OWNERS, split_axis=0, concat_axis=0, tiled=True)  5.8 us
    convert_element_type x1, other arithmetic, encode(): jnp.where(weights < 0, -level, level).astype(jnp.int32).astype(jnp.int16)  4.82 us
  transfers between devices with their start and end apart: 2, of which 2 were waited for; matrix products, arithmetic and copies ran while one was open for 1% of the time, Pallas kernels for 0%

profile of v1, /device:TPU:20, one launch (start us, length us, event | category | flops | bytes accessed | tf_op | source)
XLA Modules:
  0.0 129.7 jit_solution(12438627038119147104)
XLA Ops:
  0.7 4.8 %fusion.8 = (s16[3,4,16384]{2,1,0:T(4,128)(2,1)S(1)}, f32[3,4,16384]{2,1,0:T(4,128)}) fusion(f32[3,4,16384]{2,1,0:T(4,128)} %param.8, f32[3,4,16384]{2,1,0:T(4,128)} %param.10, bf16[3,4,16384]{2,1,0:T(4,128)(2,1)} %param.11, f32[3,4,16384]{2,1,0:T(4,128)} %param.9), kind=kLoop, calls=%fused_computation.14 | loop fusion | flops 5898240 | bytes 3932160 | tf_op jit(solution)/shard_map/convert_element_type | solution.py:47
  5.5 0.4 reshape.61
  5.9 1.2 copy.13
  7.2 16.5 %all-to-all-start = ((s16[64,3,8,128]{3,2,1,0:T(8,128)(2,1)}), s16[64,3,8,128]{3,2,1,0:T(8,128)(2,1)S(1)}, u32[]{:S(2)}, u32[]{:S(2)}) async-start(s16[64,3,8,128]{3,2,1,0:T(8,128)(2,1)} %bitcast.1), calls=%async_computation | async-start | bytes 786432 | tf_op jit(solution)/shard_map/all_to_all | solution.py:158
  23.8 0.1 fusion.9
  24.0 0.2 select_reduce_fusion.1
  24.3 0.1 reduce_sum.58
  24.5 0.1 convert_reduce_fusion.1
  24.6 0.3 convolution_convert_fusion
  24.9 0.1 reshape.63
  25.0 15.3 %all-to-all-done = s16[64,3,8,128]{3,2,1,0:T(8,128)(2,1)S(1)} async-done(((s16[64,3,8,128]{3,2,1,0:T(8,128)(2,1)}), s16[64,3,8,128]{3,2,1,0:T(8,128)(2,1)S(1)}, u32[]{:S(2)}, u32[]{:S(2)}) %all-to-all-start) | async-done | bytes 393248 | tf_op jit(solution)/shard_map/all_to_all | solution.py:158
  40.3 1.5 %broadcast_in_dim.4 = bf16[16,4,3,2048]{3,2,1,0:T(4,128)(2,1)} broadcast(bf16[16,3,2048]{2,1,0:T(4,128)(2,1)S(1)} %reshape.63), dimensions={0,2,3} | broadcast | bytes 983040 | tf_op jit(solution)/shard_map/broadcast_in_dim | solution.py:181
  41.9 5.8 %all-to-all-start.1 = ((bf16[64,3,2048]{2,1,0:T(4,128)(2,1)}), bf16[64,3,2048]{2,1,0:T(4,128)(2,1)}, u32[]{:S(2)}, u32[]{:S(2)}) async-start(bf16[64,3,2048]{2,1,0:T(4,128)(2,1)} %bitcast.3), calls=%async_computation.1 | async-start | bytes 2097152 | tf_op jit(solution)/shard_map/all_to_all | solution.py:182
  47.7 17.3 %all-gather.2 = s16[512,3,8,128]{3,2,1,0:T(8,128)(2,1)S(1)} all-gather(s16[64,3,8,128]{3,2,1,0:T(8,128)(2,1)S(1)} %all-to-all-done), channel_id=2, replica_groups=mesh['y'=8,'x'=4,'z'=8,'c'=2] {'x','c'}, dimensions={0}, use_global_device_ids=true | all-gather | bytes 3538944 | tf_op jit(solution)/shard_map/all_gather | solution.py:159
  64.9 12.0 %all-to-all-done.1 = bf16[64,3,2048]{2,1,0:T(4,128)(2,1)} async-done(((bf16[64,3,2048]{2,1,0:T(4,128)(2,1)}), bf16[64,3,2048]{2,1,0:T(4,128)(2,1)}, u32[]{:S(2)}, u32[]{:S(2)}) %all-to-all-start.1) | async-done | bytes 786464 | tf_op jit(solution)/shard_map/all_to_all | solution.py:182
  77.0 3.2 %reshape.65.tokens = bf16[192,2048]{1,0:T(8,128)(2,1)} reshape(bf16[64,3,2048]{2,1,0:T(4,128)(2,1)} %all-to-all-done.1) | data formatting | bytes 1572864 | tf_op jit(solution)/shard_map/reshape | solution.py:183
  80.1 1.1 copy-done
  81.3 7.8 %shard_map.95 = bf16[192,2048]{1,0:T(8,128)(2,1)S(1)} custom-call(s16[8,64,3,8,128]{4,3,2,1,0:T(8,128)(2,1)S(1)} %bitcast.11, bf16[192,2048]{1,0:T(8,128)(2,1)S(1)} %copy-done), custom_call_target="tpu_custom_call" | custom-call | tf_op jit(solution)/shard_map/pallas_call | solution.py:143
  89.1 0.9 copy-done.1
  90.0 2.4 %reshape.66 = bf16[64,3,2048]{2,1,0:T(4,128)(2,1)S(1)} reshape(bf16[192,2048]{1,0:T(8,128)(2,1)} %copy-done.1) | data formatting | bytes 1572864 | tf_op jit(solution)/shard_map/reshape | solution.py:185
  92.4 35.6 %all_to_all.15 = bf16[64,3,2048]{2,1,0:T(4,128)(2,1)S(1)} all-to-all(bf16[64,3,2048]{2,1,0:T(4,128)(2,1)S(1)} %reshape.66), channel_id=1, replica_groups=mesh['y'=8,'x'=4,'z'=8,'c'=2] {'y','z'}, dimensions={0} | all-to-all | bytes 1572864 | tf_op jit(solution)/shard_map/all_to_all | solution.py:186
  128.0 0.6 convert_reduce_fusion
  128.6 0.2 reshape.69
  128.8 0.9 convolution_convert_fusion.1
  (17 shorter events, 0.4 us)
Async XLA Ops:
  0.6 23.0 %copy-start.4 = (s32[4,8]{1,0:T(4,128)S(1)}, s32[4,8]{1,0:T(4,128)}, u32[]{:S(2)}) copy-start(s32[4,8]{1,0:T(4,128)} %param.14) | copy-start | bytes 388
  0.6 23.1 %copy-start.2 = (bf16[4,2048]{1,0:T(4,128)(2,1)S(1)}, bf16[4,2048]{1,0:T(4,128)(2,1)}, u32[]{:S(2)}) copy-start(bf16[4,2048]{1,0:T(4,128)(2,1)} %param.12) | copy-start | bytes 49156
  0.7 23.6 %copy-start.5 = (f32[4,8]{1,0:T(4,128)S(1)}, f32[4,8]{1,0:T(4,128)}, u32[]{:S(2)}) copy-start(f32[4,8]{1,0:T(4,128)} %param.15) | copy-start | bytes 388
  0.7 23.9 %copy-start.3 = (f32[2048]{0:T(1024)S(1)}, f32[2048]{0:T(1024)}, u32[]{:S(2)}) copy-start(f32[2048]{0:T(1024)} %param.13) | copy-start | bytes 24580
  7.2 33.1 %all-to-all-start = ((s16[64,3,8,128]{3,2,1,0:T(8,128)(2,1)}), s16[64,3,8,128]{3,2,1,0:T(8,128)(2,1)S(1)}, u32[]{:S(2)}, u32[]{:S(2)}) async-start(s16[64,3,8,128]{3,2,1,0:T(8,128)(2,1)} %bitcast.1), calls=%async_computation | async-start | bytes 786432 | tf_op jit(solution)/shard_map/all_to_all | solution.py:158
  41.9 35.1 %all-to-all-start.1 = ((bf16[64,3,2048]{2,1,0:T(4,128)(2,1)}), bf16[64,3,2048]{2,1,0:T(4,128)(2,1)}, u32[]{:S(2)}, u32[]{:S(2)}) async-start(bf16[64,3,2048]{2,1,0:T(4,128)(2,1)} %bitcast.3), calls=%async_computation.1 | async-start | bytes 2097152 | tf_op jit(solution)/shard_map/all_to_all | solution.py:182
  80.1 1.1 copy-start
  89.1 0.9 copy-start.1

commit v2 on v1

v2 whole, which is shorter than its diff:
```python
import jax
import jax.numpy as jnp
from jax import lax
from jax.experimental import pallas as pl
from jax.experimental.pallas import tpu as pltpu
from jax.sharding import Mesh, PartitionSpec as P

E = 16
TOP = 8
QBLOCK = 128
STEP = 10
CAP = 3

BETA_ONE = 0.9
BETA_TWO = 0.95
LEARN_RATE = 0.01
ADAM_EPSILON = 1e-08
WEIGHT_DECAY = 0.1
SATURATION = 448.0
SCALE_EPSILON = 1e-06
NORM_EPSILON = 1e-06
SUBNORMAL_EDGE = 0.015625

BOUND = 0.1875
LEVELS = 32767.0
UNIT = BOUND / LEVELS**5

AXES = ("yh", "yl", "x", "zh", "zl", "c")
OWNERS = ("yh", "zh", "yl", "zl")
EXPERTS = ("yh", "zh")
QUARTERS = ("yl", "zl")
HOMES = ("yl", "zl", "yh", "zh")
COPIES = ("x", "c")


def adam_tile(master, moment_one, moment_two, grad_float):
    first = BETA_ONE * moment_one + (1.0 - BETA_ONE) * grad_float
    second = BETA_TWO * moment_two + (1.0 - BETA_TWO) * grad_float * grad_float
    correct_one = 1.0 - BETA_ONE**STEP
    correct_two = 1.0 - BETA_TWO**STEP
    direction = first * (1.0 / correct_one) / (
        jnp.sqrt(second * (1.0 / correct_two)) + ADAM_EPSILON
    )
    return master - LEARN_RATE * (direction + WEIGHT_DECAY * master)


def encode(weights):
    magnitude = jnp.maximum(jnp.abs(weights) * (1.0 / BOUND), 1e-30)
    level = jnp.minimum(jnp.exp2(jnp.log2(magnitude) * 0.2) * LEVELS + 0.5, LEVELS)
    return jnp.where(weights < 0, -level, level).astype(jnp.int32).astype(jnp.int16)


def adam_kernel(master, moment_one, moment_two, gradient, updated, codes):
    for d in range(codes.shape[0]):
        left = slice(d * 256, d * 256 + 128)
        right = slice(d * 256 + 128, d * 256 + 256)
        for m in range(3):

            def tile(ref):
                return jnp.concatenate(
                    [ref[m, :, left].astype(jnp.float32), ref[m, :, right].astype(jnp.float32)],
                    axis=0,
                )

            value = adam_tile(tile(master), tile(moment_one), tile(moment_two), tile(gradient))
            updated[m, :, left] = value[0:4]
            updated[m, :, right] = value[4:8]
            codes[d, m] = encode(value)


def adam_update(master, moment_one, moment_two, gradient, owners):
    steps = 8
    columns = master.shape[2] // steps
    rows = pl.BlockSpec((3, 4, columns), lambda i: (0, 0, i))
    return pl.pallas_call(
        adam_kernel,
        grid=(steps,),
        out_shape=(
            jax.ShapeDtypeStruct(master.shape, jnp.float32),
            jax.ShapeDtypeStruct((owners, 3, 8, 128), jnp.int16),
        ),
        in_specs=[rows] * 4,
        out_specs=(rows, pl.BlockSpec((owners // steps, 3, 8, 128), lambda i: (i, 0, 0, 0))),
    )(master, moment_one, moment_two, gradient)


def rms_norm(states, norm_gain):
    values = states.astype(jnp.float32)
    mean_square = jnp.mean(values * values, axis=1, keepdims=True)
    return (values * lax.rsqrt(mean_square + NORM_EPSILON) * norm_gain[None, :]).astype(
        jnp.bfloat16
    )


def snap(q):
    scaled = q * 1048577.0
    normal = scaled - (scaled - q)
    small = (q + 24576.0) - 24576.0
    return jnp.where(jnp.abs(q) < SUBNORMAL_EDGE, small, normal)


def expert_kernel(quarter, codes, tokens, out, packed, spread):
    copies = codes.shape[0]
    xs, yhs, zhs = copies // 2, codes.shape[1], codes.shape[2]

    def extremes(step, carry):
        high, low = carry
        p = step // yhs
        yh = step % yhs
        block = codes[p, yh].astype(jnp.int32).reshape(zhs * 4, 3, 8, 128)
        return jnp.maximum(high, jnp.max(block, axis=0)), jnp.minimum(low, jnp.min(block, axis=0))

    zero = jnp.zeros((3, 8, 128), jnp.int32)
    high, low = lax.fori_loop(0, copies * yhs, extremes, (zero, zero))
    top = jnp.maximum(high, -low).astype(jnp.float32)
    sub = lax.broadcasted_iota(jnp.int32, (8, 128), 0)
    scales = []
    factors = []
    for m in range(3):
        pair = []
        for h in range(2):
            level = jnp.max(
                jnp.max(top[m, 4 * h : 4 * h + 4], axis=0, keepdims=True), axis=1, keepdims=True
            )
            square = level * level
            largest = square * square * level * UNIT
            pair.append((largest + SCALE_EPSILON) / SATURATION)
        scales.append(
            jnp.concatenate([jnp.broadcast_to(v, (1, 128)) for v in pair], axis=1)
        )
        factors.append(
            jnp.where(
                sub < 4,
                jnp.broadcast_to(UNIT / pair[0], (8, 128)),
                jnp.broadcast_to(UNIT / pair[1], (8, 128)),
            )
        )

    def quantize(m):
        factor = factors[m][None]

        def values(p, yh, yl):
            block = codes[p, yh, :, yl, :, m].reshape(zhs * 2, 8, 128)
            level = block.astype(jnp.int32).astype(jnp.float32)
            square = level * level
            q = square * square * level * factor
            return snap(jnp.clip(q, -SATURATION, SATURATION))

        def step(t, carry):
            y = t // xs
            x = t % xs
            even = values(2 * x, y // 2, y % 2)
            odd = values(2 * x + 1, y // 2, y % 2)
            first_half = (lax.broadcasted_iota(jnp.int32, even.shape, 1)) < 4
            left = jnp.where(first_half, even, pltpu.roll(odd, 4, 1))
            right = jnp.where(first_half, pltpu.roll(even, 4, 1), odd)
            rows = pl.ds(pl.multiple_of(t * 64, 64), 64)
            packed[m, rows, 0:128] = left.reshape(64, 128).astype(jnp.bfloat16)
            packed[m, rows, 128:256] = right.reshape(64, 128).astype(jnp.bfloat16)
            return carry

        lax.fori_loop(0, xs * yhs * 2, step, 0)

    for m in range(3):
        quantize(m)
    token_rows = tokens[...]
    gate_act = jnp.dot(token_rows, packed[0], preferred_element_type=jnp.float32) * scales[0]
    up_act = jnp.dot(token_rows, packed[1], preferred_element_type=jnp.float32) * scales[1]
    hidden = gate_act / (1.0 + jnp.exp(-gate_act)) * up_act * scales[2]
    partial_value = lax.dot_general(
        hidden.astype(jnp.bfloat16),
        packed[2],
        (((1,), (1,)), ((), ())),
        preferred_element_type=jnp.float32,
    )
    homes, lines = out.shape[1], out.shape[2]
    rows = partial_value.shape[0] // 4
    for r in range(4):
        for k in range(lines // CAP):
            spread[r, pl.ds(k, rows, lines // CAP), :] = partial_value[
                r * rows : (r + 1) * rows, k * 128 : (k + 1) * 128
            ]
        out[quarter[0] ^ r] = spread[r].reshape(homes, lines, 128).astype(jnp.bfloat16)


def experts(quarter, codes, tokens):
    rows, width = tokens.shape
    homes = rows // (4 * CAP)
    lines = CAP * width // 128
    vmem = pl.BlockSpec(memory_space=pltpu.VMEM)
    return pl.pallas_call(
        expert_kernel,
        out_shape=jax.ShapeDtypeStruct((4, homes, lines, 128), jnp.bfloat16),
        in_specs=[pl.BlockSpec(memory_space=pltpu.SMEM), vmem, vmem],
        out_specs=vmem,
        scratch_shapes=[
            pltpu.VMEM((3, width, 256), jnp.bfloat16),
            pltpu.VMEM((4, homes * lines, 128), jnp.float32),
        ],
        compiler_params=pltpu.CompilerParams(vmem_limit_bytes=40 * 2**20),
    )(quarter, codes, tokens)


def combine_kernel(returned, weighted, out, total):
    lines = returned.shape[2]
    width = lines // CAP
    rows = weighted.shape[0]
    weights = weighted[...]
    sums = [jnp.zeros((width, 128), jnp.float32) for _ in range(rows)]
    for e in range(returned.shape[1]):
        for j in range(CAP):
            value = jnp.zeros((width, 128), jnp.float32)
            for q in range(returned.shape[0]):
                value = value + returned[q, e, j * width : (j + 1) * width].astype(jnp.float32)
            for t in range(rows):
                slot = e * CAP + j
                sums[t] = sums[t] + weights[t : t + 1, slot : slot + 1] * value
    for t in range(rows):
        total[t * width : (t + 1) * width] = sums[t]
    for k in range(width):
        out[:, k * 128 : (k + 1) * 128] = total[pl.ds(k, rows, width), :].astype(jnp.bfloat16)


def combine(returned, weighted):
    rows = weighted.shape[0]
    width = returned.shape[2] // CAP
    vmem = pl.BlockSpec(memory_space=pltpu.VMEM)
    return pl.pallas_call(
        combine_kernel,
        out_shape=jax.ShapeDtypeStruct((rows, width * 128), jnp.bfloat16),
        in_specs=[vmem, vmem],
        out_specs=vmem,
        scratch_shapes=[pltpu.VMEM((rows * width, 128), jnp.float32)],
        compiler_params=pltpu.CompilerParams(vmem_limit_bytes=16 * 2**20),
    )(returned, weighted)


def body(master, moment_one, moment_two, gradient, states, norm_gain, routes, route_weights):
    owners = lax.axis_size(OWNERS)
    updated, codes = adam_update(master, moment_one, moment_two, gradient, owners)
    columns = lax.all_to_all(codes, OWNERS, split_axis=0, concat_axis=0, tiled=True)
    gathered_codes = lax.all_gather(columns, COPIES, axis=0, tiled=False)

    normed = rms_norm(states, norm_gain)
    weights = route_weights / jnp.sum(route_weights, axis=1, keepdims=True)
    row_count = routes.shape[0]
    group_size = owners // E
    expert_ids = routes.reshape(-1)
    onehot = (expert_ids[:, None] == jnp.arange(E, dtype=jnp.int32)[None, :]).astype(jnp.int32)
    earlier = jnp.cumsum(onehot, axis=0) - onehot
    slot_index = jnp.sum(earlier * onehot, axis=1)
    position = expert_ids * CAP + slot_index
    placed = (position[:, None] == jnp.arange(E * CAP, dtype=jnp.int32)[None, :]).astype(
        jnp.float32
    )
    placed = placed.reshape(row_count, TOP, E * CAP)
    select = jnp.sum(placed, axis=1).astype(jnp.bfloat16)
    weighted = jnp.sum(placed * weights[:, :, None], axis=1)
    gathered = lax.dot_general(
        select, normed, (((0,), (0,)), ((), ())), preferred_element_type=jnp.float32
    )
    width = normed.shape[1]
    buffer = gathered.astype(jnp.bfloat16).reshape(E, CAP, width)
    mine = lax.all_to_all(buffer, EXPERTS, split_axis=0, concat_axis=0, tiled=True)
    mine = mine.reshape(E * CAP, width)
    swap = [[(i, i ^ r) for i in range(4)] for r in range(4)]
    parts = [mine] + [lax.ppermute(mine, QUARTERS, swap[r]) for r in (1, 2, 3)]
    tokens = jnp.concatenate(parts)
    quarter = lax.axis_index(QUARTERS).astype(jnp.int32).reshape(1)

    copies = gathered_codes.shape[0]
    gathered_codes = gathered_codes.reshape(copies, 4, 4, 2, 2, 3, 8, 128)
    partial_value = experts(quarter, gathered_codes, tokens)
    lines = partial_value.shape[2]
    returned = lax.all_to_all(
        partial_value.reshape(owners, lines, 128), HOMES, split_axis=0, concat_axis=0, tiled=True
    )
    mixture = combine(returned.reshape(group_size, E, lines, 128), weighted)
    return (updated, mixture)


def solution(mesh):
    chips = Mesh(mesh.devices.reshape(4, 2, 4, 4, 2, 2), AXES)
    rows = P(None, AXES, None)
    return jax.shard_map(
        body,
        mesh=chips,
        in_specs=(rows, rows, rows, rows, P(AXES, None), P(), P(AXES, None), P(AXES, None)),
        out_specs=(rows, P(AXES, None)),
        check_vma=False,
    )
```

time: 130 us -> 128 us (0.985)
  the two profiles are of different devices: /device:TPU:20 before, /device:TPU:1 now
where the time goes in v2:
time: 128 us; the launch traced here: 126 us
  blocking collectives  52 us (41%)
  starting transfers between devices  32.4 us (25%)
  waiting for transfers between devices  19 us (15%)
  Pallas kernels  15.5 us (12%)
  other arithmetic  3.58 us (3%)
  local copies, waits for them, and re-layouts  1.84 us (1%)
    all_to_all x1, blocking collectives, body(): lax.all_to_all(partial_value.reshape(owners, lines, 128), HOMES, split_ax...  32.1 us
    all_gather x1, blocking collectives, body(): gathered_codes = lax.all_gather(columns, COPIES, axis=0, tiled=False)  19.9 us
    all_to_all x1, starting transfers between devices, body(): lax.all_to_all(buffer, EXPERTS, split_axis=0, concat_axis=0, tiled=True)  16.2 us
    ppermute x3, waiting for transfers between devices, body(): parts = [mine] + [lax.ppermute(mine, QUARTERS, swap[r]) for r in (1, 2, 3)]  12.8 us
    pallas_call x1, Pallas kernels, experts(): pl.pallas_call(expert_kernel, out_shape=jax.ShapeDtypeStruct((4, homes, l...  8.38 us
    ppermute x3, starting transfers between devices, body(): parts = [mine] + [lax.ppermute(mine, QUARTERS, swap[r]) for r in (1, 2, 3)]  8.37 us
    all_to_all x1, starting transfers between devices, body(): lax.all_to_all(codes, OWNERS, split_axis=0, concat_axis=0, tiled=True)  7.82 us
    all_to_all x1, waiting for transfers between devices, body(): lax.all_to_all(buffer, EXPERTS, split_axis=0, concat_axis=0, tiled=True)  6.2 us
  transfers between devices with their start and end apart: 5, of which 4 were waited for; matrix products, arithmetic and copies ran while one was open for 0% of the time, Pallas kernels for 5%

profile of v2, /device:TPU:1, one launch (start us, length us, event | category | flops | bytes accessed | tf_op | source)
XLA Modules:
  0.0 126.0 jit_solution(7429040821581080584)
XLA Ops:
  0.6 0.8 eq.29
  1.4 0.8 fusion
  2.3 0.8 reduce_sum.51
  3.1 0.8 broadcast_divide_fusion
  3.9 0.2 select_reduce_fusion.1
  4.2 0.7 multiply_add_fusion
  4.9 0.1 select_reduce_fusion
  5.0 1.0 convolution_convert_fusion
  6.0 0.8 reshape.54
  6.8 16.2 %all-to-all-start.1 = ((bf16[16,3,2048]{2,1,0:T(4,128)(2,1)}), bf16[16,3,2048]{2,1,0:T(4,128)(2,1)S(1)}, u32[]{:S(2)}, u32[]{:S(2)}) async-start(bf16[16,3,2048]{2,1,0:T(4,128)(2,1)} %reshape.54), calls=%async_computation.1 | async-start | bytes 524288 | tf_op jit(solution)/shard_map/all_to_all | solution.py:264
  23.0 6.1 %shard_map.95 = (f32[3,4,16384]{2,1,0:T(4,128)}, s16[64,3,8,128]{3,2,1,0:T(8,128)(2,1)}) custom-call(f32[3,4,16384]{2,1,0:T(4,128)} %master.1, f32[3,4,16384]{2,1,0:T(4,128)} %moment_one.1, f32[3,4,16384]{2,1,0:T(4,128)} %moment_two.1, bf16[3,4,16384]{2,1,0:T(4,128)(2,1)} %gradient.1), custom_call_target="tpu_custom_call" | custom-call | tf_op jit(solution)/shard_map/pallas_call | solution.py:75
  29.2 6.2 %all-to-all-done.1 = bf16[16,3,2048]{2,1,0:T(4,128)(2,1)S(1)} async-done(((bf16[16,3,2048]{2,1,0:T(4,128)(2,1)}), bf16[16,3,2048]{2,1,0:T(4,128)(2,1)S(1)}, u32[]{:S(2)}, u32[]{:S(2)}) %all-to-all-start.1) | async-done | bytes 196640 | tf_op jit(solution)/shard_map/all_to_all | solution.py:264
  35.4 7.8 %all-to-all-start = ((s16[64,3,8,128]{3,2,1,0:T(8,128)(2,1)}), s16[64,3,8,128]{3,2,1,0:T(8,128)(2,1)S(1)}, u32[]{:S(2)}, u32[]{:S(2)}) async-start(s16[64,3,8,128]{3,2,1,0:T(8,128)(2,1)} %get-tuple-element.5), calls=%async_computation | async-start | bytes 786432 | tf_op jit(solution)/shard_map/all_to_all | solution.py:241
  43.2 0.2 reshape.55
  43.4 3.8 %collective-permute-start.2 = (bf16[48,2048]{1,0:T(8,128)(2,1)S(1)}, bf16[48,2048]{1,0:T(8,128)(2,1)S(1)}, u32[]{:S(2)}, u32[]{:S(2)}) collective-permute-start(bf16[48,2048]{1,0:T(8,128)(2,1)S(1)} %reshape.55), channel_id=1, source_target_pairs={{0,66},{2,64},{64,2},{66,0},{1,67},{3,65},{65,3},{67,1},{4,70},{6,... | collective-permute-start | bytes 589832 | tf_op jit(solution)/shard_map/ppermute | solution.py:267
  47.2 2.2 %collective-permute-start.1 = (bf16[48,2048]{1,0:T(8,128)(2,1)S(1)}, bf16[48,2048]{1,0:T(8,128)(2,1)S(1)}, u32[]{:S(2)}, u32[]{:S(2)}) collective-permute-start(bf16[48,2048]{1,0:T(8,128)(2,1)S(1)} %reshape.55), channel_id=1, source_target_pairs={{0,64},{2,66},{64,0},{66,2},{1,65},{3,67},{65,1},{67,3},{4,68},{6,... | collective-permute-start | bytes 589832 | tf_op jit(solution)/shard_map/ppermute | solution.py:267
  49.4 2.4 %collective-permute-start = (bf16[48,2048]{1,0:T(8,128)(2,1)S(1)}, bf16[48,2048]{1,0:T(8,128)(2,1)S(1)}, u32[]{:S(2)}, u32[]{:S(2)}) collective-permute-start(bf16[48,2048]{1,0:T(8,128)(2,1)S(1)} %reshape.55), channel_id=1, source_target_pairs={{0,2},{2,0},{64,66},{66,64},{1,3},{3,1},{65,67},{67,65},{4,6},{6,4... | collective-permute-start | bytes 589832 | tf_op jit(solution)/shard_map/ppermute | solution.py:267
  51.8 6.9 %collective-permute-done.2 = bf16[48,2048]{1,0:T(8,128)(2,1)S(1)} collective-permute-done((bf16[48,2048]{1,0:T(8,128)(2,1)S(1)}, bf16[48,2048]{1,0:T(8,128)(2,1)S(1)}, u32[]{:S(2)}, u32[]{:S(2)}) %collective-permute-start.2) | collective-permute-done | bytes 196640 | tf_op jit(solution)/shard_map/ppermute | solution.py:267
  58.7 3.8 %collective-permute-done.1 = bf16[48,2048]{1,0:T(8,128)(2,1)S(1)} collective-permute-done((bf16[48,2048]{1,0:T(8,128)(2,1)S(1)}, bf16[48,2048]{1,0:T(8,128)(2,1)S(1)}, u32[]{:S(2)}, u32[]{:S(2)}) %collective-permute-start.1) | collective-permute-done | bytes 196640 | tf_op jit(solution)/shard_map/ppermute | solution.py:267
  62.5 2.0 %collective-permute-done = bf16[48,2048]{1,0:T(8,128)(2,1)S(1)} collective-permute-done((bf16[48,2048]{1,0:T(8,128)(2,1)S(1)}, bf16[48,2048]{1,0:T(8,128)(2,1)S(1)}, u32[]{:S(2)}, u32[]{:S(2)}) %collective-permute-start) | collective-permute-done | bytes 196640 | tf_op jit(solution)/shard_map/ppermute | solution.py:267
  64.7 19.9 %all-gather.2 = s16[512,3,8,128]{3,2,1,0:T(8,128)(2,1)S(1)} all-gather(s16[64,3,8,128]{3,2,1,0:T(8,128)(2,1)S(1)} %all-to-all-done), channel_id=2, replica_groups=mesh['yh'=4,'yl'=2,'x'=4,'zh'=4,'zl'=2,'c'=2] {'x','c'}, dimensions={0}, use_global_device_ids=true | all-gather | bytes 3538944 | tf_op jit(solution)/shard_map/all_gather | solution.py:242
  84.6 8.4 %shard_map.96 = bf16[4,16,48,128]{3,2,1,0:T(8,128)(2,1)S(1)} custom-call(s32[1]{0:T(128)} %bitcast.quarter, s16[8,4,4,2,2,3,8,128]{7,6,5,4,3,2,1,0:T(8,128)(2,1)S(1)} %bitcast.5, bf16[192,2048]{1,0:T(8,128)(2,1)S(1)} %pad_maximum_fusion.tokens), custom_call_target="tpu_custom_call" | custom-call | tf_op jit(solution)/shard_map/pallas_call | solution.py:191
  93.0 32.1 %all_to_all.15 = bf16[64,48,128]{2,1,0:T(8,128)(2,1)S(1)} all-to-all(bf16[64,48,128]{2,1,0:T(8,128)(2,1)S(1)} %bitcast.6), channel_id=1, replica_groups=mesh['yh'=4,'yl'=2,'x'=4,'zh'=4,'zl'=2,'c'=2] {'yl','zl','yh','zh'}, dimensions={0} | all-to-all | bytes 1572864 | tf_op jit(solution)/shard_map/all_to_all | solution.py:275
  125.1 1.0 shard_map.97
  (6 shorter events, 0.3 us)
Async XLA Ops:
  6.8 28.6 %all-to-all-start.1 = ((bf16[16,3,2048]{2,1,0:T(4,128)(2,1)}), bf16[16,3,2048]{2,1,0:T(4,128)(2,1)S(1)}, u32[]{:S(2)}, u32[]{:S(2)}) async-start(bf16[16,3,2048]{2,1,0:T(4,128)(2,1)} %reshape.54), calls=%async_computation.1 | async-start | bytes 524288 | tf_op jit(solution)/shard_map/all_to_all | solution.py:264
  35.4 29.2 %all-to-all-start = ((s16[64,3,8,128]{3,2,1,0:T(8,128)(2,1)}), s16[64,3,8,128]{3,2,1,0:T(8,128)(2,1)S(1)}, u32[]{:S(2)}, u32[]{:S(2)}) async-start(s16[64,3,8,128]{3,2,1,0:T(8,128)(2,1)} %get-tuple-element.5), calls=%async_computation | async-start | bytes 786432 | tf_op jit(solution)/shard_map/all_to_all | solution.py:241
  43.4 15.3 %collective-permute-start.2 = (bf16[48,2048]{1,0:T(8,128)(2,1)S(1)}, bf16[48,2048]{1,0:T(8,128)(2,1)S(1)}, u32[]{:S(2)}, u32[]{:S(2)}) collective-permute-start(bf16[48,2048]{1,0:T(8,128)(2,1)S(1)} %reshape.55), channel_id=1, source_target_pairs={{0,66},{2,64},{64,2},{66,0},{1,67},{3,65},{65,3},{67,1},{4,70},{6,... | collective-permute-start | bytes 589832 | tf_op jit(solution)/shard_map/ppermute | solution.py:267
  47.2 15.3 %collective-permute-start.1 = (bf16[48,2048]{1,0:T(8,128)(2,1)S(1)}, bf16[48,2048]{1,0:T(8,128)(2,1)S(1)}, u32[]{:S(2)}, u32[]{:S(2)}) collective-permute-start(bf16[48,2048]{1,0:T(8,128)(2,1)S(1)} %reshape.55), channel_id=1, source_target_pairs={{0,64},{2,66},{64,0},{66,2},{1,65},{3,67},{65,1},{67,3},{4,68},{6,... | collective-permute-start | bytes 589832 | tf_op jit(solution)/shard_map/ppermute | solution.py:267
  49.4 15.1 %collective-permute-start = (bf16[48,2048]{1,0:T(8,128)(2,1)S(1)}, bf16[48,2048]{1,0:T(8,128)(2,1)S(1)}, u32[]{:S(2)}, u32[]{:S(2)}) collective-permute-start(bf16[48,2048]{1,0:T(8,128)(2,1)S(1)} %reshape.55), channel_id=1, source_target_pairs={{0,2},{2,0},{64,66},{66,64},{1,3},{3,1},{65,67},{67,65},{4,6},{6,4... | collective-permute-start | bytes 589832 | tf_op jit(solution)/shard_map/ppermute | solution.py:267

commit v3 on v2

v3 whole, which is shorter than its diff:
```python
import jax
import jax.numpy as jnp
from jax import lax
from jax.experimental import pallas as pl
from jax.experimental.pallas import tpu as pltpu
from jax.sharding import Mesh, PartitionSpec as P

E = 16
TOP = 8
QBLOCK = 128
STEP = 10
CAP = 3

BETA_ONE = 0.9
BETA_TWO = 0.95
LEARN_RATE = 0.01
ADAM_EPSILON = 1e-08
WEIGHT_DECAY = 0.1
SATURATION = 448.0
SCALE_EPSILON = 1e-06
NORM_EPSILON = 1e-06

BOUND = 0.1875
LEVELS = 32767.0
UNIT = BOUND / LEVELS**5

TOKEN_BOUND = 68.0
TOKEN_UNIT = TOKEN_BOUND / LEVELS**5

AXES = ("yh", "yl", "x", "zh", "zl", "c")
OWNERS = ("yh", "zh", "yl", "zl")
COPIES = ("x", "c")


def adam_tile(master, moment_one, moment_two, grad_float):
    first = BETA_ONE * moment_one + (1.0 - BETA_ONE) * grad_float
    second = BETA_TWO * moment_two + (1.0 - BETA_TWO) * grad_float * grad_float
    correct_one = 1.0 - BETA_ONE**STEP
    correct_two = 1.0 - BETA_TWO**STEP
    mean = second * (1.0 / correct_two)
    spread = mean * lax.rsqrt(mean) + ADAM_EPSILON
    inverse = pl.reciprocal(spread, approx=True)
    inverse = inverse * (2.0 - spread * inverse)
    direction = first * (1.0 / correct_one) * inverse
    return master - LEARN_RATE * (direction + WEIGHT_DECAY * master)


def encode(values, bound):
    magnitude = jnp.maximum(jnp.abs(values) * (1.0 / bound), 1e-30)
    level = jnp.minimum(jnp.exp2(jnp.log2(magnitude) * 0.2) * LEVELS + 0.5, LEVELS)
    return jnp.where(values < 0, -level, level).astype(jnp.int32)


def dispatch(states, norm_gain, routes, route_weights, weighted, lines, chosen):
    rows, width = states.shape
    blocks = width // 128
    values = states[...].astype(jnp.float32)
    mean_square = jnp.mean(values * values, axis=1, keepdims=True)
    normed = values * lax.rsqrt(mean_square + NORM_EPSILON) * norm_gain[...]
    level = encode(normed, TOKEN_BOUND).astype(jnp.float32)
    for k in range(blocks):
        lines[pl.ds(k, rows, blocks), :] = level[:, k * 128 : (k + 1) * 128]

    lane = lax.broadcasted_iota(jnp.int32, (rows, 128), 1)
    expert = lane // CAP
    ids = routes[...]
    gains = route_weights[...]
    gains = gains / jnp.sum(gains, axis=1, keepdims=True)
    named = jnp.zeros((rows, 128), jnp.float32)
    gain = jnp.zeros((rows, 128), jnp.float32)
    for k in range(TOP):
        hit = ids[:, k : k + 1] == expert
        named = jnp.where(hit, 1.0, named)
        gain = jnp.where(hit, gains[:, k : k + 1], gain)
    slot = (lane - expert * CAP).astype(jnp.float32)
    earlier = jnp.zeros((1, 128), jnp.float32)
    picks = []
    for t in range(rows):
        pick = jnp.where(earlier == slot[t : t + 1], named[t : t + 1], 0.0)
        weighted[t : t + 1, :] = pick * gain[t : t + 1]
        picks.append(pick)
        earlier = earlier + named[t : t + 1]
    tiles = [lines[t * blocks : (t + 1) * blocks] for t in range(rows)]
    for n in range(E * CAP):
        row = picks[0][:, n : n + 1] * tiles[0]
        for t in range(1, rows):
            row = row + picks[t][:, n : n + 1] * tiles[t]
        chosen[n] = row.astype(jnp.int32).astype(jnp.int16).reshape(2, 8, 128)


def owner_kernel(
    master, moment_one, moment_two, gradient, states, norm_gain, routes, route_weights,
    updated, codes, weighted, lines, chosen,
):
    step = pl.program_id(0)

    @pl.when(step == 0)
    def _():
        dispatch(states, norm_gain, routes, route_weights, weighted, lines, chosen)

    dests = codes.shape[0]
    for d in range(dests):
        left = slice(d * 256, d * 256 + 128)
        right = slice(d * 256 + 128, d * 256 + 256)
        for m in range(3):

            def tile(ref):
                return jnp.concatenate(
                    [ref[m, :, left].astype(jnp.float32), ref[m, :, right].astype(jnp.float32)],
                    axis=0,
                )

            value = adam_tile(tile(master), tile(moment_one), tile(moment_two), tile(gradient))
            updated[m, :, left] = value[0:4]
            updated[m, :, right] = value[4:8]
            codes[d, m] = encode(value, BOUND).astype(jnp.int16)
        for j in range(CAP):
            slot = (step * (dests // 4) + d // 4) * CAP + j
            codes[d, 3 + j] = chosen[slot, d % 2]


def prepare(master, moment_one, moment_two, gradient, states, norm_gain, routes, route_weights, owners):
    steps = 2
    columns = master.shape[2] // steps
    rows = pl.BlockSpec((3, 4, columns), lambda i: (0, 0, i))
    whole = lambda array: pl.BlockSpec(array.shape, lambda i: (0, 0))
    count, width = states.shape
    small = (states, norm_gain, routes, route_weights)
    return pl.pallas_call(
        owner_kernel,
        grid=(steps,),
        out_shape=(
            jax.ShapeDtypeStruct(master.shape, jnp.float32),
            jax.ShapeDtypeStruct((owners, 3 + CAP, 8, 128), jnp.int16),
            jax.ShapeDtypeStruct((count, 128), jnp.float32),
        ),
        in_specs=[rows] * 4 + [whole(array) for array in small],
        out_specs=(
            rows,
            pl.BlockSpec((owners // steps, 3 + CAP, 8, 128), lambda i: (i, 0, 0, 0)),
            pl.BlockSpec((count, 128), lambda i: (0, 0)),
        ),
        scratch_shapes=[
            pltpu.VMEM((count * width // 128, 128), jnp.float32),
            pltpu.VMEM((E * CAP, 2, 8, 128), jnp.int16),
        ],
        compiler_params=pltpu.CompilerParams(vmem_limit_bytes=60 * 2**20),
    )(master, moment_one, moment_two, gradient, *small)


def snap(q):
    clipped = jnp.clip(q, -SATURATION, SATURATION)
    return clipped.astype(jnp.float8_e4m3fn).astype(jnp.bfloat16)


def expert_kernel(place, codes, near, far, out, packed, spread, lines):
    copies = codes.shape[0]
    xs, yhs, zhs = copies // 2, codes.shape[1], codes.shape[2]

    def extremes(step, carry):
        high, low = carry
        p = step // yhs
        yh = step % yhs
        block = codes[p, yh].astype(jnp.int32).reshape(zhs * 4, 3, 8, 128)
        return jnp.maximum(high, jnp.max(block, axis=0)), jnp.minimum(low, jnp.min(block, axis=0))

    zero = jnp.zeros((3, 8, 128), jnp.int32)
    high, low = lax.fori_loop(0, copies * yhs, extremes, (zero, zero), unroll=4)
    top = jnp.maximum(high, -low).astype(jnp.float32)
    sub = lax.broadcasted_iota(jnp.int32, (8, 128), 0)
    scales = []
    factors = []
    for m in range(3):
        pair = []
        for h in range(2):
            level = jnp.max(
                jnp.max(top[m, 4 * h : 4 * h + 4], axis=0, keepdims=True), axis=1, keepdims=True
            )
            square = level * level
            largest = square * square * level * UNIT
            pair.append((largest + SCALE_EPSILON) / SATURATION)
        scales.append(
            jnp.concatenate([jnp.broadcast_to(v, (1, 128)) for v in pair], axis=1)
        )
        factors.append(
            jnp.where(
                sub < 4,
                jnp.broadcast_to(UNIT / pair[0], (8, 128)),
                jnp.broadcast_to(UNIT / pair[1], (8, 128)),
            )
        )

    def quantize(m):
        factor = factors[m][None]

        def values(p, yh, yl):
            block = codes[p, yh, :, yl, :, m].reshape(zhs * 2, 8, 128)
            level = block.astype(jnp.int32).astype(jnp.float32)
            square = level * level
            q = square * square * level * factor
            return q

        def step(t, carry):
            y = t // xs
            x = t % xs
            even = values(2 * x, y // 2, y % 2)
            odd = values(2 * x + 1, y // 2, y % 2)
            first_half = (lax.broadcasted_iota(jnp.int32, even.shape, 1)) < 4
            left = jnp.where(first_half, even, pltpu.roll(odd, 4, 1))
            right = jnp.where(first_half, pltpu.roll(even, 4, 1), odd)
            rows = pl.ds(pl.multiple_of(t * 64, 64), 64)
            packed[m, rows, 0:128] = snap(left.reshape(64, 128))
            packed[m, rows, 128:256] = snap(right.reshape(64, 128))
            return carry

        lax.fori_loop(0, xs * yhs * 2, step, 0, unroll=4)

    for m in range(3):
        quantize(m)
    gate_act = jnp.zeros((lines.shape[0] // 8, 256), jnp.float32)
    up_act = jnp.zeros((lines.shape[0] // 8, 256), jnp.float32)
    half = packed.shape[1] // 2
    for part, own in ((near, place[0]), (far, 1 - place[0])):
        level = part[...].astype(jnp.int32).astype(jnp.float32)
        square = level * level
        lines[...] = (square * square * level * TOKEN_UNIT).reshape(lines.shape)
        token_rows = jnp.concatenate(
            [lines[pl.ds(k, lines.shape[0] // 8, 8), :].astype(jnp.bfloat16) for k in range(8)], axis=1
        )
        features = pl.ds(pl.multiple_of(own * half, half), half)
        gate_act += jnp.dot(token_rows, packed[0, features], preferred_element_type=jnp.float32)
        up_act += jnp.dot(token_rows, packed[1, features], preferred_element_type=jnp.float32)
    gate_act = gate_act * scales[0]
    up_act = up_act * scales[1]
    hidden = gate_act / (1.0 + jnp.exp(-gate_act)) * up_act * scales[2]
    partial_value = lax.dot_general(
        hidden.astype(jnp.bfloat16),
        packed[2],
        (((1,), (1,)), ((), ())),
        preferred_element_type=jnp.float32,
    )
    rows = partial_value.shape[0]
    for k in range(out.shape[1] // CAP):
        spread[pl.ds(k, rows, out.shape[1] // CAP), :] = partial_value[:, k * 128 : (k + 1) * 128]
    out[...] = spread[...].reshape(out.shape).astype(jnp.bfloat16)


def experts(place, codes, near, far):
    sources = near.shape[0]
    width = 2 * 8 * 128
    lines = CAP * width // 128
    vmem = pl.BlockSpec(memory_space=pltpu.VMEM)
    return pl.pallas_call(
        expert_kernel,
        out_shape=jax.ShapeDtypeStruct((sources, lines, 128), jnp.bfloat16),
        in_specs=[pl.BlockSpec(memory_space=pltpu.SMEM), vmem, vmem, vmem],
        out_specs=vmem,
        scratch_shapes=[
            pltpu.VMEM((3, width, 256), jnp.bfloat16),
            pltpu.VMEM((sources * lines, 128), jnp.float32),
            pltpu.VMEM((sources * CAP * 8, 128), jnp.float32),
        ],
        compiler_params=pltpu.CompilerParams(vmem_limit_bytes=40 * 2**20),
    )(place, codes, near, far)


def combine_kernel(returned, weighted, out, total):
    lines = returned.shape[2]
    width = lines // CAP
    rows = weighted.shape[0]
    weights = weighted[...]
    sums = [jnp.zeros((width, 128), jnp.float32) for _ in range(rows)]
    for e in range(returned.shape[0]):
        for j in range(CAP):
            value = jnp.zeros((width, 128), jnp.float32)
            for q in range(returned.shape[1]):
                value = value + returned[e, q, j * width : (j + 1) * width].astype(jnp.float32)
            for t in range(rows):
                slot = e * CAP + j
                sums[t] = sums[t] + weights[t : t + 1, slot : slot + 1] * value
    for t in range(rows):
        total[t * width : (t + 1) * width] = sums[t]
    for k in range(width):
        out[:, k * 128 : (k + 1) * 128] = total[pl.ds(k, rows, width), :].astype(jnp.bfloat16)


def combine(returned, weighted):
    rows = weighted.shape[0]
    width = returned.shape[2] // CAP
    vmem = pl.BlockSpec(memory_space=pltpu.VMEM)
    return pl.pallas_call(
        combine_kernel,
        out_shape=jax.ShapeDtypeStruct((rows, width * 128), jnp.bfloat16),
        in_specs=[vmem, vmem],
        out_specs=vmem,
        scratch_shapes=[pltpu.VMEM((rows * width, 128), jnp.float32)],
        compiler_params=pltpu.CompilerParams(vmem_limit_bytes=16 * 2**20),
    )(returned, weighted)


def body(master, moment_one, moment_two, gradient, states, norm_gain, routes, route_weights):
    owners = lax.axis_size(OWNERS)
    updated, codes, weighted = prepare(
        master, moment_one, moment_two, gradient, states, norm_gain[None, :], routes, route_weights, owners
    )
    received = lax.all_to_all(codes, OWNERS, split_axis=0, concat_axis=0, tiled=True)
    near = received[:, 3:]
    far = lax.ppermute(near, "zl", [(0, 1), (1, 0)])
    gathered = lax.all_gather(received[:, :3], COPIES, axis=0, tiled=False)
    place = lax.axis_index("zl").astype(jnp.int32).reshape(1)
    partial_value = experts(place, gathered.reshape(-1, 4, 4, 2, 2, 3, 8, 128), near, far)
    returned = lax.all_to_all(partial_value, OWNERS, split_axis=0, concat_axis=0, tiled=True)
    mixture = combine(returned.reshape(E, owners // E, -1, 128), weighted)
    return (updated, mixture)


def solution(mesh):
    chips = Mesh(mesh.devices.reshape(4, 2, 4, 4, 2, 2), AXES)
    rows = P(None, AXES, None)
    return jax.shard_map(
        body,
        mesh=chips,
        in_specs=(rows, rows, rows, rows, P(AXES, None), P(), P(AXES, None), P(AXES, None)),
        out_specs=(rows, P(AXES, None)),
        check_vma=False,
    )
```

time: 128 us -> 105 us (0.82)
  starting transfers between devices: 32.4 us -> 19.2 us
  Pallas kernels: 15.5 us -> 10.5 us
  other arithmetic: 3.58 us -> 0 us
  waiting for transfers between devices: 19 us -> 22 us
  local copies, waits for them, and re-layouts: 1.84 us -> 0.08 us
    all_to_all x1, waiting for transfers between devices: 0.01 us -> 22 us  [body(): lax.all_to_all(codes, OWNERS, split_axis=0, concat_axis=0, tiled=True)]
    all_to_all x1 -> x0, starting transfers between devices: 16.2 us -> none  [body(): lax.all_to_all(buffer, EXPERTS, split_axis=0, concat_axis=0, tiled=True)]
    ppermute x3 -> x1, waiting for transfers between devices: 12.8 us -> 0.01 us  [body(): far = lax.ppermute(near, 'zl', [(0, 1), (1, 0)])]
    all_to_all x1, starting transfers between devices: 7.82 us -> 17.1 us  [body(): lax.all_to_all(codes, OWNERS, split_axis=0, concat_axis=0, tiled=True)]
    ppermute x3 -> x1, starting transfers between devices: 8.37 us -> 2.11 us  [body(): far = lax.ppermute(near, 'zl', [(0, 1), (1, 0)])]
    all_to_all x1 -> x0, waiting for transfers between devices: 6.2 us -> none  [body(): lax.all_to_all(buffer, EXPERTS, split_axis=0, concat_axis=0, tiled=True)]
    pallas_call x2, Pallas kernels: 14.5 us -> 9.5 us  [the longest x1 5.55 us: experts(): pl.pallas_call(expert_kernel, out_shape=jax.ShapeDtypeStruct((sources, li...]
    all_to_all x1, blocking collectives: 32.1 us -> 29.6 us  [body(): lax.all_to_all(partial_value, OWNERS, split_axis=0, concat_axis=0, tiled=...]
  transfers between devices with their start and end apart: 5 -> 2, of which waited for: 4 -> 1; matrix products, arithmetic and copies ran while one was open for 0% -> 0% of each run, Pallas kernels for 5% -> 0%
where the time goes in v3:
time: 105 us; the launch traced here: 104 us
  blocking collectives  51.7 us (49%)
  waiting for transfers between devices  22 us (21%)
  starting transfers between devices  19.2 us (18%)
  Pallas kernels  10.5 us (10%)
    all_to_all x1, blocking collectives, body(): lax.all_to_all(partial_value, OWNERS, split_axis=0, concat_axis=0, tiled=...  29.6 us
    all_gather x1, blocking collectives, body(): gathered = lax.all_gather(received[:, :3], COPIES, axis=0, tiled=False)  22.1 us
    all_to_all x1, waiting for transfers between devices, body(): lax.all_to_all(codes, OWNERS, split_axis=0, concat_axis=0, tiled=True)  22 us
    all_to_all x1, starting transfers between devices, body(): lax.all_to_all(codes, OWNERS, split_axis=0, concat_axis=0, tiled=True)  17.1 us
    pallas_call x1, Pallas kernels, experts(): pl.pallas_call(expert_kernel, out_shape=jax.ShapeDtypeStruct((sources, li...  5.55 us
    pallas_call x1, Pallas kernels, prepare(): pl.pallas_call(owner_kernel, grid=(steps,), out_shape=(jax.ShapeDtypeStru...  3.95 us
    ppermute x1, starting transfers between devices, body(): far = lax.ppermute(near, 'zl', [(0, 1), (1, 0)])  2.11 us
  transfers between devices with their start and end apart: 2, of which 1 were waited for; matrix products, arithmetic and copies ran while one was open for 0% of the time, Pallas kernels for 0%

profile of v3, /device:TPU:1, one launch (start us, length us, event | category | flops | bytes accessed | tf_op | source)
XLA Modules:
  0.0 104.2 jit_solution(15887639556357238045)
XLA Ops:
  0.6 3.9 %shard_map.95 = (f32[3,4,16384]{2,1,0:T(4,128)}, s16[64,6,8,128]{3,2,1,0:T(8,128)(2,1)}, f32[4,128]{1,0:T(4,128)}) custom-call(f32[3,4,16384]{2,1,0:T(4,128)} %master.1, f32[3,4,16384]{2,1,0:T(4,128)} %moment_one.1, f32[3,4,16384]{2,1,0:T(4,128)} %moment_two.1, bf16[3,4,16384]{2,1,0:T(4,128)(2,1)} %gradient.1, bf16[4,2048]{1,0:T(4,128)(2,1)} %states.1, ...), custom_call_target="tpu_custom_call" | custom-call | tf_op jit(solution)/shard_map/pallas_call | solution.py:129
  4.6 17.1 %all-to-all-start = ((s16[64,6,8,128]{3,2,1,0:T(8,128)(2,1)}), s16[64,6,8,128]{3,2,1,0:T(8,128)(2,1)S(1)}, u32[]{:S(2)}, u32[]{:S(2)}) async-start(s16[64,6,8,128]{3,2,1,0:T(8,128)(2,1)} %get-tuple-element.6), calls=%async_computation | async-start | bytes 1572864 | tf_op jit(solution)/shard_map/all_to_all | solution.py:306
  21.7 22.0 %all-to-all-done = s16[64,6,8,128]{3,2,1,0:T(8,128)(2,1)S(1)} async-done(((s16[64,6,8,128]{3,2,1,0:T(8,128)(2,1)}), s16[64,6,8,128]{3,2,1,0:T(8,128)(2,1)S(1)}, u32[]{:S(2)}, u32[]{:S(2)}) %all-to-all-start) | async-done | bytes 786464 | tf_op jit(solution)/shard_map/all_to_all | solution.py:306
  43.7 0.1 fusion
  43.8 2.1 %collective-permute-start = (s16[64,3,8,128]{3,2,1,0:T(8,128)(2,1)S(1)}, s16[64,3,8,128]{3,2,1,0:T(8,128)(2,1)S(1)}, u32[]{:S(2)}, u32[]{:S(2)}) collective-permute-start(s16[64,3,8,128]{3,2,1,0:T(8,128)(2,1)S(1)} %get-tuple-element.8.near), channel_id=1, source_target_pairs={{0,2},{2,0},{1,3},{3,1},{4,6},{6,4},{5,7},{7,5},{8,10},{10,8},{9,1... | collective-permute-start | bytes 1179656 | tf_op jit(solution)/shard_map/ppermute | solution.py:308
  45.9 22.1 %all-gather.2 = s16[512,3,8,128]{3,2,1,0:T(8,128)(2,1)S(1)} all-gather(s16[64,3,8,128]{3,2,1,0:T(8,128)(2,1)S(1)} %get-tuple-element.9), channel_id=2, replica_groups=mesh['yh'=4,'yl'=2,'x'=4,'zh'=4,'zl'=2,'c'=2] {'x','c'}, dimensions={0}, use_global_device_ids=true | all-gather | bytes 3538944 | tf_op jit(solution)/shard_map/all_gather | solution.py:309
  68.0 0.0 collective-permute-done.far
  68.0 0.0 copy-start
  68.0 5.6 %shard_map.96 = bf16[64,48,128]{2,1,0:T(8,128)(2,1)S(1)} custom-call(s32[1]{0:T(128)} %bitcast.1.place, s16[8,4,4,2,2,3,8,128]{7,6,5,4,3,2,1,0:T(8,128)(2,1)S(1)} %bitcast.4, s16[64,3,8,128]{3,2,1,0:T(8,128)(2,1)S(1)} %get-tuple-element.8.near, s16[64,3,8,128]{3,2,1,0:T(8,128)(2,1)S(1)} %collective-permute-done.far), custom_call_target="tpu_custom_call" | custom-call | tf_op jit(solution)/shard_map/pallas_call | solution.py:253
  73.6 29.6 %all_to_all.10 = bf16[64,48,128]{2,1,0:T(8,128)(2,1)S(1)} all-to-all(bf16[64,48,128]{2,1,0:T(8,128)(2,1)S(1)} %shard_map.96), channel_id=1, replica_groups=mesh['yh'=4,'yl'=2,'x'=4,'zh'=4,'zl'=2,'c'=2] {'yh','zh','yl','zl'}, dimensions={0} | all-to-all | bytes 1572864 | tf_op jit(solution)/shard_map/all_to_all | solution.py:312
  103.2 0.0 copy-done
  103.2 1.0 shard_map.97
Async XLA Ops:
  4.6 39.1 %all-to-all-start = ((s16[64,6,8,128]{3,2,1,0:T(8,128)(2,1)}), s16[64,6,8,128]{3,2,1,0:T(8,128)(2,1)S(1)}, u32[]{:S(2)}, u32[]{:S(2)}) async-start(s16[64,6,8,128]{3,2,1,0:T(8,128)(2,1)} %get-tuple-element.6), calls=%async_computation | async-start | bytes 1572864 | tf_op jit(solution)/shard_map/all_to_all | solution.py:306
  43.8 24.2 %collective-permute-start = (s16[64,3,8,128]{3,2,1,0:T(8,128)(2,1)S(1)}, s16[64,3,8,128]{3,2,1,0:T(8,128)(2,1)S(1)}, u32[]{:S(2)}, u32[]{:S(2)}) collective-permute-start(s16[64,3,8,128]{3,2,1,0:T(8,128)(2,1)S(1)} %get-tuple-element.8.near), channel_id=1, source_target_pairs={{0,2},{2,0},{1,3},{3,1},{4,6},{6,4},{5,7},{7,5},{8,10},{10,8},{9,1... | collective-permute-start | bytes 1179656 | tf_op jit(solution)/shard_map/ppermute | solution.py:308
  68.0 35.2 %copy-start = (f32[4,128]{1,0:T(4,128)S(1)}, f32[4,128]{1,0:T(4,128)}, u32[]{:S(2)}) copy-start(f32[4,128]{1,0:T(4,128)} %get-tuple-element.7.weighted) | copy-start | bytes 6148

commit v4 on v3

--- a/solution.py
+++ b/solution.py
@@ -26,6 +26,8 @@
 
 TOKEN_BOUND = 68.0
 TOKEN_UNIT = TOKEN_BOUND / LEVELS**5
+ACT_BOUND = 524288.0
+ACT_UNIT = ACT_BOUND / LEVELS**7
 
 AXES = ("yh", "yl", "x", "zh", "zl", "c")
 OWNERS = ("yh", "zh", "yl", "zl")
@@ -45,9 +47,9 @@
     return master - LEARN_RATE * (direction + WEIGHT_DECAY * master)
 
 
-def encode(values, bound):
-    magnitude = jnp.maximum(jnp.abs(values) * (1.0 / bound), 1e-30)
-    level = jnp.minimum(jnp.exp2(jnp.log2(magnitude) * 0.2) * LEVELS + 0.5, LEVELS)
+def encode(values, bound, power=5):
+    magnitude = jnp.maximum(jnp.abs(values) * (1.0 / bound), 1e-35)
+    level = jnp.minimum(jnp.exp2(jnp.log2(magnitude) * (1.0 / power)) * LEVELS + 0.5, LEVELS)
     return jnp.where(values < 0, -level, level).astype(jnp.int32)
 
 
@@ -99,6 +101,8 @@
         dispatch(states, norm_gain, routes, route_weights, weighted, lines, chosen)
 
     dests = codes.shape[0]
+    pair_rows = lax.broadcasted_iota(jnp.int32, (8, 128), 0) % 4 < 2
+    down = []
     for d in range(dests):
         left = slice(d * 256, d * 256 + 128)
         right = slice(d * 256 + 128, d * 256 + 256)
@@ -113,7 +117,16 @@
             value = adam_tile(tile(master), tile(moment_one), tile(moment_two), tile(gradient))
             updated[m, :, left] = value[0:4]
             updated[m, :, right] = value[4:8]
-            codes[d, m] = encode(value, BOUND).astype(jnp.int16)
+            if m < 2:
+                codes[d, m] = encode(value, BOUND).astype(jnp.int16)
+            else:
+                down.append(encode(value, BOUND))
+        if d % 2:
+            first, second = down[d - 1], down[d]
+            low = jnp.where(pair_rows, first, pltpu.roll(second, 2, 0))
+            high = jnp.where(pair_rows, pltpu.roll(first, 6, 0), second)
+            codes[d - 1, 2] = low.astype(jnp.int16)
+            codes[d, 2] = high.astype(jnp.int16)
         for j in range(CAP):
             slot = (step * (dests // 4) + d // 4) * CAP + j
             codes[d, 3 + j] = chosen[slot, d % 2]
@@ -153,9 +166,23 @@
     return clipped.astype(jnp.float8_e4m3fn).astype(jnp.bfloat16)
 
 
-def expert_kernel(place, codes, near, far, out, packed, spread, lines):
+def level_value(level, unit):
+    square = level * level
+    return square * square * level * unit
+
+
+def block_level(top, rows):
+    return jnp.max(jnp.max(top[rows], axis=0, keepdims=True), axis=1, keepdims=True)
+
+
+def scale_of(level):
+    return (level_value(level, UNIT) + SCALE_EPSILON) / SATURATION
+
+
+def gate_kernel(place, codes, near, far, out, packed, lines):
     copies = codes.shape[0]
     xs, yhs, zhs = copies // 2, codes.shape[1], codes.shape[2]
+    rows = near.shape[0] * CAP
 
     def extremes(step, carry):
         high, low = carry
@@ -170,35 +197,18 @@
     sub = lax.broadcasted_iota(jnp.int32, (8, 128), 0)
     scales = []
     factors = []
-    for m in range(3):
-        pair = []
-        for h in range(2):
-            level = jnp.max(
-                jnp.max(top[m, 4 * h : 4 * h + 4], axis=0, keepdims=True), axis=1, keepdims=True
-            )
-            square = level * level
-            largest = square * square * level * UNIT
-            pair.append((largest + SCALE_EPSILON) / SATURATION)
-        scales.append(
-            jnp.concatenate([jnp.broadcast_to(v, (1, 128)) for v in pair], axis=1)
-        )
-        factors.append(
-            jnp.where(
-                sub < 4,
-                jnp.broadcast_to(UNIT / pair[0], (8, 128)),
-                jnp.broadcast_to(UNIT / pair[1], (8, 128)),
-            )
-        )
+    for m in range(2):
+        pair = [scale_of(block_level(top[m], slice(4 * h, 4 * h + 4))) for h in range(2)]
+        scales.append(jnp.concatenate([jnp.broadcast_to(v, (1, 128)) for v in pair], axis=1))
+        wide = [jnp.broadcast_to(UNIT / v, (8, 128)) for v in pair]
+        factors.append(jnp.where(sub < 4, wide[0], wide[1]))
 
     def quantize(m):
         factor = factors[m][None]
 
         def values(p, yh, yl):
             block = codes[p, yh, :, yl, :, m].reshape(zhs * 2, 8, 128)
-            level = block.astype(jnp.int32).astype(jnp.float32)
-            square = level * level
-            q = square * square * level * factor
-            return q
+            return level_value(block.astype(jnp.int32).astype(jnp.float32), factor)
 
         def step(t, carry):
             y = t // xs
@@ -208,92 +218,174 @@
             first_half = (lax.broadcasted_iota(jnp.int32, even.shape, 1)) < 4
             left = jnp.where(first_half, even, pltpu.roll(odd, 4, 1))
             right = jnp.where(first_half, pltpu.roll(even, 4, 1), odd)
-            rows = pl.ds(pl.multiple_of(t * 64, 64), 64)
-            packed[m, rows, 0:128] = snap(left.reshape(64, 128))
-            packed[m, rows, 128:256] = snap(right.reshape(64, 128))
+            span = pl.ds(pl.multiple_of(t * 64, 64), 64)
+            packed[m, span, 0:128] = snap(left.reshape(64, 128))
+            packed[m, span, 128:256] = snap(right.reshape(64, 128))
             return carry
 
         lax.fori_loop(0, xs * yhs * 2, step, 0, unroll=4)
 
-    for m in range(3):
+    for m in range(2):
         quantize(m)
-    gate_act = jnp.zeros((lines.shape[0] // 8, 256), jnp.float32)
-    up_act = jnp.zeros((lines.shape[0] // 8, 256), jnp.float32)
+    gate_act = jnp.zeros((rows, 256), jnp.float32)
+    up_act = jnp.zeros((rows, 256), jnp.float32)
     half = packed.shape[1] // 2
     for part, own in ((near, place[0]), (far, 1 - place[0])):
         level = part[...].astype(jnp.int32).astype(jnp.float32)
-        square = level * level
-        lines[...] = (square * square * level * TOKEN_UNIT).reshape(lines.shape)
+        lines[...] = level_value(level, TOKEN_UNIT).reshape(lines.shape)
         token_rows = jnp.concatenate(
-            [lines[pl.ds(k, lines.shape[0] // 8, 8), :].astype(jnp.bfloat16) for k in range(8)], axis=1
+            [lines[pl.ds(k, rows, 8), :].astype(jnp.bfloat16) for k in range(8)], axis=1
         )
         features = pl.ds(pl.multiple_of(own * half, half), half)
         gate_act += jnp.dot(token_rows, packed[0, features], preferred_element_type=jnp.float32)
         up_act += jnp.dot(token_rows, packed[1, features], preferred_element_type=jnp.float32)
     gate_act = gate_act * scales[0]
     up_act = up_act * scales[1]
-    hidden = gate_act / (1.0 + jnp.exp(-gate_act)) * up_act * scales[2]
-    partial_value = lax.dot_general(
-        hidden.astype(jnp.bfloat16),
-        packed[2],
-        (((1,), (1,)), ((), ())),
-        preferred_element_type=jnp.float32,
-    )
-    rows = partial_value.shape[0]
-    for k in range(out.shape[1] // CAP):
-        spread[pl.ds(k, rows, out.shape[1] // CAP), :] = partial_value[:, k * 128 : (k + 1) * 128]
-    out[...] = spread[...].reshape(out.shape).astype(jnp.bfloat16)
-
-
-def experts(place, codes, near, far):
+    act = gate_act / (1.0 + jnp.exp(-gate_act)) * up_act
+    out[0:rows] = encode(act, ACT_BOUND, 7).astype(jnp.int16)
+    levels = [block_level(top[2], slice(2 * b, 2 * b + 2)) for b in range(4)]
+    line = jnp.concatenate([jnp.broadcast_to(v, (16, 64)) for v in levels], axis=1)
+    out[rows : rows + 16] = line.astype(jnp.int32).astype(jnp.int16)
+
+
+def gate_up(place, codes, near, far):
     sources = near.shape[0]
     width = 2 * 8 * 128
-    lines = CAP * width // 128
     vmem = pl.BlockSpec(memory_space=pltpu.VMEM)
     return pl.pallas_call(
-        expert_kernel,
-        out_shape=jax.ShapeDtypeStruct((sources, lines, 128), jnp.bfloat16),
+        gate_kernel,
+        out_shape=jax.ShapeDtypeStruct((sources * CAP + 16, 256), jnp.int16),
         in_specs=[pl.BlockSpec(memory_space=pltpu.SMEM), vmem, vmem, vmem],
         out_specs=vmem,
         scratch_shapes=[
-            pltpu.VMEM((3, width, 256), jnp.bfloat16),
-            pltpu.VMEM((sources * lines, 128), jnp.float32),
+            pltpu.VMEM((2, width, 256), jnp.bfloat16),
             pltpu.VMEM((sources * CAP * 8, 128), jnp.float32),
         ],
-        compiler_params=pltpu.CompilerParams(vmem_limit_bytes=40 * 2**20),
+        compiler_params=pltpu.CompilerParams(vmem_limit_bytes=20 * 2**20),
     )(place, codes, near, far)
 
 
+def down_kernel(codes, acts, out, packed, spread):
+    copies = codes.shape[0]
+    xs, yhs, zhs = copies // 2, codes.shape[1], codes.shape[2]
+    rows = acts.shape[1] - 16
+    sub = lax.broadcasted_iota(jnp.int32, (8, 128), 0)
+    marks = acts[:, rows : rows + 16].astype(jnp.int32).astype(jnp.float32)
+    line = jnp.max(jnp.maximum(marks[0], marks[1]), axis=0, keepdims=True)
+    level = acts[:, 0:rows].astype(jnp.int32).astype(jnp.float32)
+    square = level * level
+    act = (square * square * square * level * ACT_UNIT).astype(jnp.bfloat16)
+    scales = [None] * 4
+    factor = jnp.zeros((8, 128), jnp.float32)
+    for h in range(2):
+        for t in range(2):
+            b = 2 * h + t
+            scale = scale_of(jnp.max(line[:, b * 64 : (b + 1) * 64], axis=1, keepdims=True))
+            scales[2 * t + h] = scale
+            factor = jnp.where(sub // 2 == b, jnp.broadcast_to(UNIT / scale, (8, 128)), factor)
+    factor = factor[None]
+    low_pair = (lax.broadcasted_iota(jnp.int32, (zhs, 8, 128), 1)) % 4 < 2
+    low_half = (lax.broadcasted_iota(jnp.int32, (zhs, 8, 128), 1)) < 4
+
+    def values(p, yh, yl, zl):
+        block = codes[p, yh, :, yl, zl, 2]
+        return level_value(block.astype(jnp.int32).astype(jnp.float32), factor)
+
+    def step(i, carry):
+        y = i // xs
+        x = i % xs
+        yh, yl = y // 2, y % 2
+        by_t = []
+        for zl in range(2):
+            even = values(2 * x, yh, yl, zl)
+            odd = values(2 * x + 1, yh, yl, zl)
+            by_t.append(
+                (
+                    jnp.where(low_pair, even, pltpu.roll(odd, 2, 1)),
+                    jnp.where(low_pair, pltpu.roll(even, 6, 1), odd),
+                )
+            )
+        span = pl.ds(pl.multiple_of(i * zhs * 8, zhs * 8), zhs * 8)
+        for t in range(2):
+            near, far = by_t[0][t], by_t[1][t]
+            top = jnp.where(low_half, near, pltpu.roll(far, 4, 1))
+            bottom = jnp.where(low_half, pltpu.roll(near, 4, 1), far)
+            packed[span, 256 * t : 256 * t + 128] = snap(top.reshape(zhs * 8, 128))
+            packed[span, 256 * t + 128 : 256 * t + 256] = snap(bottom.reshape(zhs * 8, 128))
+        return carry
+
+    lax.fori_loop(0, xs * yhs * 2, step, 0, unroll=4)
+    partial_value = jnp.zeros((rows, packed.shape[0]), jnp.float32)
+    for b in range(4):
+        partial_value += scales[b] * lax.dot_general(
+            act[b // 2, :, 128 * (b % 2) : 128 * (b % 2) + 128],
+            packed[:, 128 * b : 128 * b + 128],
+            (((1,), (1,)), ((), ())),
+            preferred_element_type=jnp.float32,
+        )
+    blocks = out.shape[1] // CAP
+    for k in range(blocks):
+        spread[pl.ds(k, rows, blocks), :] = partial_value[:, k * 128 : (k + 1) * 128]
+    out[...] = spread[...].reshape(out.shape).astype(jnp.bfloat16)
+
+
+def down(codes, acts):
+    sources = (acts.shape[1] - 16) // CAP
+    lines = CAP * 8
+    vmem = pl.BlockSpec(memory_space=pltpu.VMEM)
+    return pl.pallas_call(
+        down_kernel,
+        out_shape=jax.ShapeDtypeStruct((sources, lines, 128), jnp.bfloat16),
+        in_specs=[vmem, vmem],
+        out_specs=vmem,
+        scratch_shapes=[
+            pltpu.VMEM((lines // CAP * 128, 512), jnp.bfloat16),
+            pltpu.VMEM((sources * lines, 128), jnp.float32),
+        ],
+        compiler_params=pltpu.CompilerParams(vmem_limit_bytes=20 * 2**20),
+    )(codes, acts)
+
+
 def combine_kernel(returned, weighted, out, total):
-    lines = returned.shape[2]
+    experts, lines = returned.shape[0], returned.shape[3]
     width = lines // CAP
     rows = weighted.shape[0]
     weights = weighted[...]
-    sums = [jnp.zeros((width, 128), jnp.float32) for _ in range(rows)]
-    for e in range(returned.shape[0]):
+    sums = [[jnp.zeros((width, 128), jnp.float32) for _ in range(rows)] for _ in range(2)]
+    for e in range(experts):
         for j in range(CAP):
-            value = jnp.zeros((width, 128), jnp.float32)
-            for q in range(returned.shape[1]):
-                value = value + returned[e, q, j * width : (j + 1) * width].astype(jnp.float32)
-            for t in range(rows):
-                slot = e * CAP + j
-                sums[t] = sums[t] + weights[t : t + 1, slot : slot + 1] * value
-    for t in range(rows):
-        total[t * width : (t + 1) * width] = sums[t]
+            slot = e * CAP + j
+            for zl in range(2):
+                value = returned[e, 0, zl, j * width : (j + 1) * width].astype(jnp.float32)
+                value = value + returned[e, 1, zl, j * width : (j + 1) * width].astype(jnp.float32)
+                for t in range(rows):
+                    sums[zl][t] = sums[zl][t] + weights[t : t + 1, slot : slot + 1] * value
+    source = lax.broadcasted_iota(jnp.int32, (128, 256), 0)
+    target = lax.broadcasted_iota(jnp.int32, (128, 256), 1)
+    placed = jnp.zeros((rows * width, 256), jnp.float32)
+    for zl in range(2):
+        spot = (target == source // 2 * 4 + 2 * zl + source % 2).astype(jnp.float32).astype(jnp.bfloat16)
+        halves = jnp.concatenate(sums[zl], axis=0).astype(jnp.bfloat16)
+        placed += jnp.dot(halves, spot, preferred_element_type=jnp.float32)
+    total[0] = placed[:, 0:128]
+    total[1] = placed[:, 128:256]
     for k in range(width):
-        out[:, k * 128 : (k + 1) * 128] = total[pl.ds(k, rows, width), :].astype(jnp.bfloat16)
+        for h in range(2):
+            out[:, k * 256 + h * 128 : k * 256 + h * 128 + 128] = total[
+                h, pl.ds(k, rows, width), :
+            ].astype(jnp.bfloat16)
 
 
 def combine(returned, weighted):
     rows = weighted.shape[0]
-    width = returned.shape[2] // CAP
+    width = returned.shape[3] // CAP
     vmem = pl.BlockSpec(memory_space=pltpu.VMEM)
     return pl.pallas_call(
         combine_kernel,
-        out_shape=jax.ShapeDtypeStruct((rows, width * 128), jnp.bfloat16),
+        out_shape=jax.ShapeDtypeStruct((rows, width * 256), jnp.bfloat16),
         in_specs=[vmem, vmem],
         out_specs=vmem,
-        scratch_shapes=[pltpu.VMEM((rows * width, 128), jnp.float32)],
+        scratch_shapes=[pltpu.VMEM((2, rows * width, 128), jnp.float32)],
         compiler_params=pltpu.CompilerParams(vmem_limit_bytes=16 * 2**20),
     )(returned, weighted)
 
@@ -308,9 +400,11 @@
     far = lax.ppermute(near, "zl", [(0, 1), (1, 0)])
     gathered = lax.all_gather(received[:, :3], COPIES, axis=0, tiled=False)
     place = lax.axis_index("zl").astype(jnp.int32).reshape(1)
-    partial_value = experts(place, gathered.reshape(-1, 4, 4, 2, 2, 3, 8, 128), near, far)
+    gathered = gathered.reshape(-1, 4, 4, 2, 2, 3, 8, 128)
+    acts = lax.all_gather(gate_up(place, gathered, near, far), "zl", axis=0, tiled=False)
+    partial_value = down(gathered, acts)
     returned = lax.all_to_all(partial_value, OWNERS, split_axis=0, concat_axis=0, tiled=True)
-    mixture = combine(returned.reshape(E, owners // E, -1, 128), weighted)
+    mixture = combine(returned.reshape(E, 2, 2, -1, 128), weighted)
     return (updated, mixture)
 
 

time: 105 us -> 103 us (0.981)
  blocking collectives: 51.7 us -> 48.6 us
    all_to_all x1, blocking collectives: 29.6 us -> 21.4 us  [body(): lax.all_to_all(partial_value, OWNERS, split_axis=0, concat_axis=0, tiled=...]
    all_gather x0 -> x1, blocking collectives: none -> 5.1 us  [body(): lax.all_gather(gate_up(place, gathered, near, far), 'zl', axis=0, tiled=F...]
    pallas_call x1 -> x2, Pallas kernels: 5.55 us -> 5.95 us  [the longest x1 4.09 us: gate_up(): pl.pallas_call(gate_kernel, out_shape=jax.ShapeDtypeStruct((sources * CAP...]
where the time goes in v4:
time: 103 us; the launch traced here: 102 us
  blocking collectives  48.6 us (47%)
  waiting for transfers between devices  22 us (21%)
  starting transfers between devices  19.2 us (19%)
  Pallas kernels  11 us (11%)
    all_gather x1, blocking collectives, body(): gathered = lax.all_gather(received[:, :3], COPIES, axis=0, tiled=False)  22.1 us
    all_to_all x1, waiting for transfers between devices, body(): lax.all_to_all(codes, OWNERS, split_axis=0, concat_axis=0, tiled=True)  22 us
    all_to_all x1, blocking collectives, body(): lax.all_to_all(partial_value, OWNERS, split_axis=0, concat_axis=0, tiled=...  21.4 us
    all_to_all x1, starting transfers between devices, body(): lax.all_to_all(codes, OWNERS, split_axis=0, concat_axis=0, tiled=True)  17.1 us
    all_gather x1, blocking collectives, body(): lax.all_gather(gate_up(place, gathered, near, far), 'zl', axis=0, tiled=F...  5.1 us
    pallas_call x1, Pallas kernels, gate_up(): pl.pallas_call(gate_kernel, out_shape=jax.ShapeDtypeStruct((sources * CAP...  4.09 us
    pallas_call x1, Pallas kernels, prepare(): pl.pallas_call(owner_kernel, grid=(steps,), out_shape=(jax.ShapeDtypeStru...  3.97 us
    ppermute x1, starting transfers between devices, body(): far = lax.ppermute(near, 'zl', [(0, 1), (1, 0)])  2.11 us
  transfers between devices with their start and end apart: 2, of which 1 were waited for; matrix products, arithmetic and copies ran while one was open for 0% of the time, Pallas kernels for 0%

profile of v4, /device:TPU:1, one launch (start us, length us, event | category | flops | bytes accessed | tf_op | source)
XLA Modules:
  0.0 101.6 jit_solution(3766465222386816027)
XLA Ops:
  0.6 4.0 %shard_map.95 = (f32[3,4,16384]{2,1,0:T(4,128)}, s16[64,6,8,128]{3,2,1,0:T(8,128)(2,1)}, f32[4,128]{1,0:T(4,128)}) custom-call(f32[3,4,16384]{2,1,0:T(4,128)} %master.1, f32[3,4,16384]{2,1,0:T(4,128)} %moment_one.1, f32[3,4,16384]{2,1,0:T(4,128)} %moment_two.1, bf16[3,4,16384]{2,1,0:T(4,128)(2,1)} %gradient.1, bf16[4,2048]{1,0:T(4,128)(2,1)} %states.1, ...), custom_call_target="tpu_custom_call" | custom-call | tf_op jit(solution)/shard_map/pallas_call | solution.py:142
  4.6 17.1 %all-to-all-start = ((s16[64,6,8,128]{3,2,1,0:T(8,128)(2,1)}), s16[64,6,8,128]{3,2,1,0:T(8,128)(2,1)S(1)}, u32[]{:S(2)}, u32[]{:S(2)}) async-start(s16[64,6,8,128]{3,2,1,0:T(8,128)(2,1)} %get-tuple-element.6), calls=%async_computation | async-start | bytes 1572864 | tf_op jit(solution)/shard_map/all_to_all | solution.py:398
  21.7 22.0 %all-to-all-done = s16[64,6,8,128]{3,2,1,0:T(8,128)(2,1)S(1)} async-done(((s16[64,6,8,128]{3,2,1,0:T(8,128)(2,1)}), s16[64,6,8,128]{3,2,1,0:T(8,128)(2,1)S(1)}, u32[]{:S(2)}, u32[]{:S(2)}) %all-to-all-start) | async-done | bytes 786464 | tf_op jit(solution)/shard_map/all_to_all | solution.py:398
  43.7 0.1 fusion
  43.8 2.1 %collective-permute-start = (s16[64,3,8,128]{3,2,1,0:T(8,128)(2,1)S(1)}, s16[64,3,8,128]{3,2,1,0:T(8,128)(2,1)S(1)}, u32[]{:S(2)}, u32[]{:S(2)}) collective-permute-start(s16[64,3,8,128]{3,2,1,0:T(8,128)(2,1)S(1)} %get-tuple-element.8.near), channel_id=1, source_target_pairs={{0,2},{2,0},{1,3},{3,1},{4,6},{6,4},{5,7},{7,5},{8,10},{10,8},{9,1... | collective-permute-start | bytes 1179656 | tf_op jit(solution)/shard_map/ppermute | solution.py:400
  45.9 22.1 %all-gather.3 = s16[512,3,8,128]{3,2,1,0:T(8,128)(2,1)S(1)} all-gather(s16[64,3,8,128]{3,2,1,0:T(8,128)(2,1)S(1)} %get-tuple-element.9), channel_id=2, replica_groups=mesh['yh'=4,'yl'=2,'x'=4,'zh'=4,'zl'=2,'c'=2] {'x','c'}, dimensions={0}, use_global_device_ids=true | all-gather | bytes 3538944 | tf_op jit(solution)/shard_map/all_gather | solution.py:401
  68.1 0.0 collective-permute-done.far
  68.1 4.1 %shard_map.96 = s16[208,256]{1,0:T(8,128)(2,1)S(1)} custom-call(s32[1]{0:T(128)} %bitcast.2.place, s16[8,4,4,2,2,3,8,128]{7,6,5,4,3,2,1,0:T(8,128)(2,1)S(1)} %bitcast.5, s16[64,3,8,128]{3,2,1,0:T(8,128)(2,1)S(1)} %get-tuple-element.8.near, s16[64,3,8,128]{3,2,1,0:T(8,128)(2,1)S(1)} %collective-permute-done.far), custom_call_target="tpu_custom_call" | custom-call | tf_op jit(solution)/shard_map/pallas_call | solution.py:255
  72.2 0.0 copy-start
  72.2 5.1 %all-gather.1 = s16[416,256]{1,0:T(8,128)(2,1)S(1)} all-gather(s16[208,256]{1,0:T(8,128)(2,1)S(1)} %shard_map.96), channel_id=3, replica_groups=mesh['yh'=4,'yl'=2,'x'=4,'zh'=4,'zl'=2,'c'=2] {'zl'}, dimensions={0}, use_global_device_ids=true | all-gather | bytes 319488 | tf_op jit(solution)/shard_map/all_gather | solution.py:404
  77.3 1.9 %shard_map.97 = bf16[64,24,128]{2,1,0:T(8,128)(2,1)S(1)} custom-call(s16[8,4,4,2,2,3,8,128]{7,6,5,4,3,2,1,0:T(8,128)(2,1)S(1)} %bitcast.6, s16[2,208,256]{2,1,0:T(8,128)(2,1)S(1)} %bitcast.8), custom_call_target="tpu_custom_call" | custom-call | tf_op jit(solution)/shard_map/pallas_call | solution.py:336
  79.1 21.4 %all_to_all.10 = bf16[64,24,128]{2,1,0:T(8,128)(2,1)S(1)} all-to-all(bf16[64,24,128]{2,1,0:T(8,128)(2,1)S(1)} %shard_map.97), channel_id=1, replica_groups=mesh['yh'=4,'yl'=2,'x'=4,'zh'=4,'zl'=2,'c'=2] {'yh','zh','yl','zl'}, dimensions={0} | all-to-all | bytes 786432 | tf_op jit(solution)/shard_map/all_to_all | solution.py:406
  100.5 0.0 copy-done
  100.5 1.1 %shard_map.98 = bf16[4,2048]{1,0:T(4,128)(2,1)} custom-call(bf16[16,2,2,24,128]{4,3,2,1,0:T(8,128)(2,1)S(1)} %bitcast.7, f32[4,128]{1,0:T(4,128)S(1)} %copy-done), custom_call_target="tpu_custom_call" | custom-call | tf_op jit(solution)/shard_map/pallas_call | solution.py:383
Async XLA Ops:
  4.6 39.1 %all-to-all-start = ((s16[64,6,8,128]{3,2,1,0:T(8,128)(2,1)}), s16[64,6,8,128]{3,2,1,0:T(8,128)(2,1)S(1)}, u32[]{:S(2)}, u32[]{:S(2)}) async-start(s16[64,6,8,128]{3,2,1,0:T(8,128)(2,1)} %get-tuple-element.6), calls=%async_computation | async-start | bytes 1572864 | tf_op jit(solution)/shard_map/all_to_all | solution.py:398
  43.8 24.2 %collective-permute-start = (s16[64,3,8,128]{3,2,1,0:T(8,128)(2,1)S(1)}, s16[64,3,8,128]{3,2,1,0:T(8,128)(2,1)S(1)}, u32[]{:S(2)}, u32[]{:S(2)}) collective-permute-start(s16[64,3,8,128]{3,2,1,0:T(8,128)(2,1)S(1)} %get-tuple-element.8.near), channel_id=1, source_target_pairs={{0,2},{2,0},{1,3},{3,1},{4,6},{6,4},{5,7},{7,5},{8,10},{10,8},{9,1... | collective-permute-start | bytes 1179656 | tf_op jit(solution)/shard_map/ppermute | solution.py:400
  72.2 28.4 %copy-start = (f32[4,128]{1,0:T(4,128)S(1)}, f32[4,128]{1,0:T(4,128)}, u32[]{:S(2)}) copy-start(f32[4,128]{1,0:T(4,128)} %get-tuple-element.7.weighted) | copy-start | bytes 6148

commit v5 on v4

--- a/solution.py
+++ b/solution.py
@@ -35,16 +35,16 @@
 
 
 def adam_tile(master, moment_one, moment_two, grad_float):
-    first = BETA_ONE * moment_one + (1.0 - BETA_ONE) * grad_float
-    second = BETA_TWO * moment_two + (1.0 - BETA_TWO) * grad_float * grad_float
-    correct_one = 1.0 - BETA_ONE**STEP
-    correct_two = 1.0 - BETA_TWO**STEP
-    mean = second * (1.0 / correct_two)
-    spread = mean * lax.rsqrt(mean) + ADAM_EPSILON
+    correct_one = LEARN_RATE / (1.0 - BETA_ONE**STEP)
+    correct_two = 1.0 / (1.0 - BETA_TWO**STEP)
+    first = (BETA_ONE * correct_one) * moment_one + ((1.0 - BETA_ONE) * correct_one) * grad_float
+    second = (BETA_TWO * correct_two) * moment_two + (
+        ((1.0 - BETA_TWO) * correct_two) * grad_float * grad_float
+    )
+    spread = second * lax.rsqrt(second) + ADAM_EPSILON
     inverse = pl.reciprocal(spread, approx=True)
     inverse = inverse * (2.0 - spread * inverse)
-    direction = first * (1.0 / correct_one) * inverse
-    return master - LEARN_RATE * (direction + WEIGHT_DECAY * master)
+    return (1.0 - LEARN_RATE * WEIGHT_DECAY) * master - first * inverse
 
 
 def encode(values, bound, power=5):
@@ -100,42 +100,40 @@
     def _():
         dispatch(states, norm_gain, routes, route_weights, weighted, lines, chosen)
 
-    dests = codes.shape[0]
     pair_rows = lax.broadcasted_iota(jnp.int32, (8, 128), 0) % 4 < 2
-    down = []
-    for d in range(dests):
-        left = slice(d * 256, d * 256 + 128)
-        right = slice(d * 256 + 128, d * 256 + 256)
-        for m in range(3):
-
-            def tile(ref):
-                return jnp.concatenate(
-                    [ref[m, :, left].astype(jnp.float32), ref[m, :, right].astype(jnp.float32)],
-                    axis=0,
+    group = 8
+
+    def some(i, carry):
+        down = []
+        for d in range(group):
+            owner = i * group + d
+            for m in range(3):
+                value = adam_tile(
+                    master[m, owner], moment_one[m, owner], moment_two[m, owner],
+                    gradient[m, owner].astype(jnp.float32),
                 )
-
-            value = adam_tile(tile(master), tile(moment_one), tile(moment_two), tile(gradient))
-            updated[m, :, left] = value[0:4]
-            updated[m, :, right] = value[4:8]
-            if m < 2:
-                codes[d, m] = encode(value, BOUND).astype(jnp.int16)
-            else:
-                down.append(encode(value, BOUND))
-        if d % 2:
-            first, second = down[d - 1], down[d]
-            low = jnp.where(pair_rows, first, pltpu.roll(second, 2, 0))
-            high = jnp.where(pair_rows, pltpu.roll(first, 6, 0), second)
-            codes[d - 1, 2] = low.astype(jnp.int16)
-            codes[d, 2] = high.astype(jnp.int16)
-        for j in range(CAP):
-            slot = (step * (dests // 4) + d // 4) * CAP + j
-            codes[d, 3 + j] = chosen[slot, d % 2]
+                updated[m, owner] = value
+                if m < 2:
+                    codes[owner, m] = encode(value, BOUND).astype(jnp.int16)
+                else:
+                    down.append(encode(value, BOUND))
+            if d % 2:
+                first, second = down[d - 1], down[d]
+                low = jnp.where(pair_rows, first, pltpu.roll(second, 2, 0))
+                high = jnp.where(pair_rows, pltpu.roll(first, 6, 0), second)
+                codes[owner - 1, 2] = low.astype(jnp.int16)
+                codes[owner, 2] = high.astype(jnp.int16)
+            slot = (step * (codes.shape[0] // 4) + i * (group // 4) + d // 4) * CAP
+            for j in range(CAP):
+                codes[owner, 3 + j] = chosen[slot + j, d % 2]
+        return carry
+
+    lax.fori_loop(0, codes.shape[0] // group, some, 0)
 
 
 def prepare(master, moment_one, moment_two, gradient, states, norm_gain, routes, route_weights, owners):
     steps = 2
-    columns = master.shape[2] // steps
-    rows = pl.BlockSpec((3, 4, columns), lambda i: (0, 0, i))
+    rows = pl.BlockSpec((3, owners // steps, 8, 128), lambda i: (0, i, 0, 0))
     whole = lambda array: pl.BlockSpec(array.shape, lambda i: (0, 0))
     count, width = states.shape
     small = (states, norm_gain, routes, route_weights)
@@ -161,6 +159,18 @@
     )(master, moment_one, moment_two, gradient, *small)
 
 
+def to_tiles(array):
+    matrices, rows, columns = array.shape
+    parts = array.reshape(matrices, rows, columns // 256, 2, 128).transpose(0, 2, 3, 1, 4)
+    return parts.reshape(matrices, columns // 256, 2 * rows, 128)
+
+
+def from_tiles(tiles):
+    matrices, owners = tiles.shape[:2]
+    parts = tiles.reshape(matrices, owners, 2, 4, 128).transpose(0, 3, 1, 2, 4)
+    return parts.reshape(matrices, 4, owners * 256)
+
+
 def snap(q):
     clipped = jnp.clip(q, -SATURATION, SATURATION)
     return clipped.astype(jnp.float8_e4m3fn).astype(jnp.bfloat16)
@@ -223,7 +233,7 @@
             packed[m, span, 128:256] = snap(right.reshape(64, 128))
             return carry
 
-        lax.fori_loop(0, xs * yhs * 2, step, 0, unroll=4)
+        lax.fori_loop(0, xs * yhs * 2, step, 0, unroll=xs * yhs * 2)
 
     for m in range(2):
         quantize(m)
@@ -314,7 +324,7 @@
             packed[span, 256 * t + 128 : 256 * t + 256] = snap(bottom.reshape(zhs * 8, 128))
         return carry
 
-    lax.fori_loop(0, xs * yhs * 2, step, 0, unroll=4)
+    lax.fori_loop(0, xs * yhs * 2, step, 0, unroll=8)
     partial_value = jnp.zeros((rows, packed.shape[0]), jnp.float32)
     for b in range(4):
         partial_value += scales[b] * lax.dot_general(
@@ -392,8 +402,9 @@
 
 def body(master, moment_one, moment_two, gradient, states, norm_gain, routes, route_weights):
     owners = lax.axis_size(OWNERS)
+    state = [to_tiles(array) for array in (master, moment_one, moment_two, gradient)]
     updated, codes, weighted = prepare(
-        master, moment_one, moment_two, gradient, states, norm_gain[None, :], routes, route_weights, owners
+        *state, states, norm_gain[None, :], routes, route_weights, owners
     )
     received = lax.all_to_all(codes, OWNERS, split_axis=0, concat_axis=0, tiled=True)
     near = received[:, 3:]
@@ -405,7 +416,7 @@
     partial_value = down(gathered, acts)
     returned = lax.all_to_all(partial_value, OWNERS, split_axis=0, concat_axis=0, tiled=True)
     mixture = combine(returned.reshape(E, 2, 2, -1, 128), weighted)
-    return (updated, mixture)
+    return (from_tiles(updated), mixture)
 
 
 def solution(mesh):

time: 103 us -> 102 us (level)
  no operation moved by 1% of the time
where the time goes in v5:
time: 102 us; the launch traced here: 101 us
  blocking collectives  48.6 us (48%)
  waiting for transfers between devices  22 us (22%)
  starting transfers between devices  19.2 us (19%)
  Pallas kernels  10.3 us (10%)
    all_gather x1, blocking collectives, body(): gathered = lax.all_gather(received[:, :3], COPIES, axis=0, tiled=False)  22.1 us
    all_to_all x1, waiting for transfers between devices, body(): lax.all_to_all(codes, OWNERS, split_axis=0, concat_axis=0, tiled=True)  22 us
    all_to_all x1, blocking collectives, body(): lax.all_to_all(partial_value, OWNERS, split_axis=0, concat_axis=0, tiled=...  21.4 us
    all_to_all x1, starting transfers between devices, body(): lax.all_to_all(codes, OWNERS, split_axis=0, concat_axis=0, tiled=True)  17.1 us
    all_gather x1, blocking collectives, body(): lax.all_gather(gate_up(place, gathered, near, far), 'zl', axis=0, tiled=F...  5.11 us
    pallas_call x1, Pallas kernels, prepare(): pl.pallas_call(owner_kernel, grid=(steps,), out_shape=(jax.ShapeDtypeStru...  3.77 us
    pallas_call x1, Pallas kernels, gate_up(): pl.pallas_call(gate_kernel, out_shape=jax.ShapeDtypeStruct((sources * CAP...  3.6 us
    ppermute x1, starting transfers between devices, body(): far = lax.ppermute(near, 'zl', [(0, 1), (1, 0)])  2.11 us
  transfers between devices with their start and end apart: 2, of which 1 were waited for; matrix products, arithmetic and copies ran while one was open for 0% of the time, Pallas kernels for 0%

profile of v5, /device:TPU:1, one launch (start us, length us, event | category | flops | bytes accessed | tf_op | source)
XLA Modules:
  0.0 100.9 jit_solution(9370437542016745443)
XLA Ops:
  0.6 3.8 %shard_map.95 = (f32[3,64,8,128]{3,2,1,0:T(8,128)}, s16[64,6,8,128]{3,2,1,0:T(8,128)(2,1)}, f32[4,128]{1,0:T(4,128)}) custom-call(f32[3,64,8,128]{3,2,1,0:T(8,128)} %bitcast.34, f32[3,64,8,128]{3,2,1,0:T(8,128)} %bitcast.35, f32[3,64,8,128]{3,2,1,0:T(8,128)} %bitcast.36, bf16[3,64,8,128]{3,2,1,0:T(8,128)(2,1)} %bitcast.37, bf16[4,2048]{1,0:T(4,128)(2,1)} %states.1, ...), custom_call_target="tpu_custom_call" | custom-call | tf_op jit(solution)/shard_map/pallas_call | solution.py:140
  4.4 17.1 %all-to-all-start = ((s16[64,6,8,128]{3,2,1,0:T(8,128)(2,1)}), s16[64,6,8,128]{3,2,1,0:T(8,128)(2,1)S(1)}, u32[]{:S(2)}, u32[]{:S(2)}) async-start(s16[64,6,8,128]{3,2,1,0:T(8,128)(2,1)} %get-tuple-element.6), calls=%async_computation | async-start | bytes 1572864 | tf_op jit(solution)/shard_map/all_to_all | solution.py:409
  21.6 22.0 %all-to-all-done = s16[64,6,8,128]{3,2,1,0:T(8,128)(2,1)S(1)} async-done(((s16[64,6,8,128]{3,2,1,0:T(8,128)(2,1)}), s16[64,6,8,128]{3,2,1,0:T(8,128)(2,1)S(1)}, u32[]{:S(2)}, u32[]{:S(2)}) %all-to-all-start) | async-done | bytes 786464 | tf_op jit(solution)/shard_map/all_to_all | solution.py:409
  43.6 0.1 fusion
  43.6 2.1 %collective-permute-start = (s16[64,3,8,128]{3,2,1,0:T(8,128)(2,1)S(1)}, s16[64,3,8,128]{3,2,1,0:T(8,128)(2,1)S(1)}, u32[]{:S(2)}, u32[]{:S(2)}) collective-permute-start(s16[64,3,8,128]{3,2,1,0:T(8,128)(2,1)S(1)} %get-tuple-element.8.near), channel_id=1, source_target_pairs={{0,2},{2,0},{1,3},{3,1},{4,6},{6,4},{5,7},{7,5},{8,10},{10,8},{9,1... | collective-permute-start | bytes 1179656 | tf_op jit(solution)/shard_map/ppermute | solution.py:411
  45.7 22.1 %all-gather.3 = s16[512,3,8,128]{3,2,1,0:T(8,128)(2,1)S(1)} all-gather(s16[64,3,8,128]{3,2,1,0:T(8,128)(2,1)S(1)} %get-tuple-element.9), channel_id=2, replica_groups=mesh['yh'=4,'yl'=2,'x'=4,'zh'=4,'zl'=2,'c'=2] {'x','c'}, dimensions={0}, use_global_device_ids=true | all-gather | bytes 3538944 | tf_op jit(solution)/shard_map/all_gather | solution.py:412
  67.9 0.0 collective-permute-done.far
  67.9 3.6 %shard_map.96 = s16[208,256]{1,0:T(8,128)(2,1)S(1)} custom-call(s32[1]{0:T(128)} %bitcast.17.place, s16[8,4,4,2,2,3,8,128]{7,6,5,4,3,2,1,0:T(8,128)(2,1)S(1)} %bitcast.30, s16[64,3,8,128]{3,2,1,0:T(8,128)(2,1)S(1)} %get-tuple-element.8.near, s16[64,3,8,128]{3,2,1,0:T(8,128)(2,1)S(1)} %collective-permute-done.far), custom_call_target="tpu_custom_call" | custom-call | tf_op jit(solution)/shard_map/pallas_call | solution.py:265
  71.5 0.0 copy-start
  71.5 5.1 %all-gather.1 = s16[416,256]{1,0:T(8,128)(2,1)S(1)} all-gather(s16[208,256]{1,0:T(8,128)(2,1)S(1)} %shard_map.96), channel_id=3, replica_groups=mesh['yh'=4,'yl'=2,'x'=4,'zh'=4,'zl'=2,'c'=2] {'zl'}, dimensions={0}, use_global_device_ids=true | all-gather | bytes 319488 | tf_op jit(solution)/shard_map/all_gather | solution.py:415
  76.6 1.8 %shard_map.97 = bf16[64,24,128]{2,1,0:T(8,128)(2,1)S(1)} custom-call(s16[8,4,4,2,2,3,8,128]{7,6,5,4,3,2,1,0:T(8,128)(2,1)S(1)} %bitcast.31, s16[2,208,256]{2,1,0:T(8,128)(2,1)S(1)} %bitcast.33), custom_call_target="tpu_custom_call" | custom-call | tf_op jit(solution)/shard_map/pallas_call | solution.py:346
  78.4 21.4 %all_to_all.10 = bf16[64,24,128]{2,1,0:T(8,128)(2,1)S(1)} all-to-all(bf16[64,24,128]{2,1,0:T(8,128)(2,1)S(1)} %shard_map.97), channel_id=1, replica_groups=mesh['yh'=4,'yl'=2,'x'=4,'zh'=4,'zl'=2,'c'=2] {'yh','zh','yl','zl'}, dimensions={0} | all-to-all | bytes 786432 | tf_op jit(solution)/shard_map/all_to_all | solution.py:417
  99.8 0.0 copy-done
  99.8 1.1 %shard_map.98 = bf16[4,2048]{1,0:T(4,128)(2,1)} custom-call(bf16[16,2,2,24,128]{4,3,2,1,0:T(8,128)(2,1)S(1)} %bitcast.32, f32[4,128]{1,0:T(4,128)S(1)} %copy-done), custom_call_target="tpu_custom_call" | custom-call | tf_op jit(solution)/shard_map/pallas_call | solution.py:393
Async XLA Ops:
  4.4 39.1 %all-to-all-start = ((s16[64,6,8,128]{3,2,1,0:T(8,128)(2,1)}), s16[64,6,8,128]{3,2,1,0:T(8,128)(2,1)S(1)}, u32[]{:S(2)}, u32[]{:S(2)}) async-start(s16[64,6,8,128]{3,2,1,0:T(8,128)(2,1)} %get-tuple-element.6), calls=%async_computation | async-start | bytes 1572864 | tf_op jit(solution)/shard_map/all_to_all | solution.py:409
  43.6 24.2 %collective-permute-start = (s16[64,3,8,128]{3,2,1,0:T(8,128)(2,1)S(1)}, s16[64,3,8,128]{3,2,1,0:T(8,128)(2,1)S(1)}, u32[]{:S(2)}, u32[]{:S(2)}) collective-permute-start(s16[64,3,8,128]{3,2,1,0:T(8,128)(2,1)S(1)} %get-tuple-element.8.near), channel_id=1, source_target_pairs={{0,2},{2,0},{1,3},{3,1},{4,6},{6,4},{5,7},{7,5},{8,10},{10,8},{9,1... | collective-permute-start | bytes 1179656 | tf_op jit(solution)/shard_map/ppermute | solution.py:411
  71.5 28.3 %copy-start = (f32[4,128]{1,0:T(4,128)S(1)}, f32[4,128]{1,0:T(4,128)}, u32[]{:S(2)}) copy-start(f32[4,128]{1,0:T(4,128)} %get-tuple-element.7.weighted) | copy-start | bytes 6148

commit v6 on v5

--- a/solution.py
+++ b/solution.py
@@ -202,7 +202,7 @@
         return jnp.maximum(high, jnp.max(block, axis=0)), jnp.minimum(low, jnp.min(block, axis=0))
 
     zero = jnp.zeros((3, 8, 128), jnp.int32)
-    high, low = lax.fori_loop(0, copies * yhs, extremes, (zero, zero), unroll=4)
+    high, low = lax.fori_loop(0, copies * yhs, extremes, (zero, zero), unroll=32)
     top = jnp.maximum(high, -low).astype(jnp.float32)
     sub = lax.broadcasted_iota(jnp.int32, (8, 128), 0)
     scales = []
@@ -235,11 +235,8 @@
 
         lax.fori_loop(0, xs * yhs * 2, step, 0, unroll=xs * yhs * 2)
 
-    for m in range(2):
-        quantize(m)
-    gate_act = jnp.zeros((rows, 256), jnp.float32)
-    up_act = jnp.zeros((rows, 256), jnp.float32)
     half = packed.shape[1] // 2
+    parts = []
     for part, own in ((near, place[0]), (far, 1 - place[0])):
         level = part[...].astype(jnp.int32).astype(jnp.float32)
         lines[...] = level_value(level, TOKEN_UNIT).reshape(lines.shape)
@@ -247,8 +244,15 @@
             [lines[pl.ds(k, rows, 8), :].astype(jnp.bfloat16) for k in range(8)], axis=1
         )
         features = pl.ds(pl.multiple_of(own * half, half), half)
-        gate_act += jnp.dot(token_rows, packed[0, features], preferred_element_type=jnp.float32)
-        up_act += jnp.dot(token_rows, packed[1, features], preferred_element_type=jnp.float32)
+        parts.append((token_rows, features))
+    sums = []
+    for m in range(2):
+        quantize(m)
+        act = jnp.zeros((rows, 256), jnp.float32)
+        for token_rows, features in parts:
+            act += jnp.dot(token_rows, packed[m, features], preferred_element_type=jnp.float32)
+        sums.append(act)
+    gate_act, up_act = sums
     gate_act = gate_act * scales[0]
     up_act = up_act * scales[1]
     act = gate_act / (1.0 + jnp.exp(-gate_act)) * up_act
@@ -324,7 +328,7 @@
             packed[span, 256 * t + 128 : 256 * t + 256] = snap(bottom.reshape(zhs * 8, 128))
         return carry
 
-    lax.fori_loop(0, xs * yhs * 2, step, 0, unroll=8)
+    lax.fori_loop(0, xs * yhs * 2, step, 0, unroll=32)
     partial_value = jnp.zeros((rows, packed.shape[0]), jnp.float32)
     for b in range(4):
         partial_value += scales[b] * lax.dot_general(

time: 102 us -> 102 us (level)
  no operation moved by 1% of the time
where the time goes in v6:
time: 102 us; the launch traced here: 101 us
  blocking collectives  48.6 us (48%)
  waiting for transfers between devices  22 us (22%)
  starting transfers between devices  19.2 us (19%)
  Pallas kernels  9.96 us (10%)
    all_gather x1, blocking collectives, body(): gathered = lax.all_gather(received[:, :3], COPIES, axis=0, tiled=False)  22.1 us
    all_to_all x1, waiting for transfers between devices, body(): lax.all_to_all(codes, OWNERS, split_axis=0, concat_axis=0, tiled=True)  22 us
    all_to_all x1, blocking collectives, body(): lax.all_to_all(partial_value, OWNERS, split_axis=0, concat_axis=0, tiled=...  21.4 us
    all_to_all x1, starting transfers between devices, body(): lax.all_to_all(codes, OWNERS, split_axis=0, concat_axis=0, tiled=True)  17.1 us
    all_gather x1, blocking collectives, body(): lax.all_gather(gate_up(place, gathered, near, far), 'zl', axis=0, tiled=F...  5.11 us
    pallas_call x1, Pallas kernels, prepare(): pl.pallas_call(owner_kernel, grid=(steps,), out_shape=(jax.ShapeDtypeStru...  3.77 us
    pallas_call x1, Pallas kernels, gate_up(): pl.pallas_call(gate_kernel, out_shape=jax.ShapeDtypeStruct((sources * CAP...  3.49 us
    ppermute x1, starting transfers between devices, body(): far = lax.ppermute(near, 'zl', [(0, 1), (1, 0)])  2.11 us
  transfers between devices with their start and end apart: 2, of which 1 were waited for; matrix products, arithmetic and copies ran while one was open for 0% of the time, Pallas kernels for 0%

profile of v6, /device:TPU:1, one launch (start us, length us, event | category | flops | bytes accessed | tf_op | source)
XLA Modules:
  0.0 100.6 jit_solution(17341764857864026040)
XLA Ops:
  0.6 3.8 %shard_map.95 = (f32[3,64,8,128]{3,2,1,0:T(8,128)}, s16[64,6,8,128]{3,2,1,0:T(8,128)(2,1)}, f32[4,128]{1,0:T(4,128)}) custom-call(f32[3,64,8,128]{3,2,1,0:T(8,128)} %bitcast.34, f32[3,64,8,128]{3,2,1,0:T(8,128)} %bitcast.35, f32[3,64,8,128]{3,2,1,0:T(8,128)} %bitcast.36, bf16[3,64,8,128]{3,2,1,0:T(8,128)(2,1)} %bitcast.37, bf16[4,2048]{1,0:T(4,128)(2,1)} %states.1, ...), custom_call_target="tpu_custom_call" | custom-call | tf_op jit(solution)/shard_map/pallas_call | solution.py:140
  4.4 17.1 %all-to-all-start = ((s16[64,6,8,128]{3,2,1,0:T(8,128)(2,1)}), s16[64,6,8,128]{3,2,1,0:T(8,128)(2,1)S(1)}, u32[]{:S(2)}, u32[]{:S(2)}) async-start(s16[64,6,8,128]{3,2,1,0:T(8,128)(2,1)} %get-tuple-element.6), calls=%async_computation | async-start | bytes 1572864 | tf_op jit(solution)/shard_map/all_to_all | solution.py:413
  21.6 22.0 %all-to-all-done = s16[64,6,8,128]{3,2,1,0:T(8,128)(2,1)S(1)} async-done(((s16[64,6,8,128]{3,2,1,0:T(8,128)(2,1)}), s16[64,6,8,128]{3,2,1,0:T(8,128)(2,1)S(1)}, u32[]{:S(2)}, u32[]{:S(2)}) %all-to-all-start) | async-done | bytes 786464 | tf_op jit(solution)/shard_map/all_to_all | solution.py:413
  43.6 0.1 fusion
  43.6 2.1 %collective-permute-start = (s16[64,3,8,128]{3,2,1,0:T(8,128)(2,1)S(1)}, s16[64,3,8,128]{3,2,1,0:T(8,128)(2,1)S(1)}, u32[]{:S(2)}, u32[]{:S(2)}) collective-permute-start(s16[64,3,8,128]{3,2,1,0:T(8,128)(2,1)S(1)} %get-tuple-element.8.near), channel_id=1, source_target_pairs={{0,2},{2,0},{1,3},{3,1},{4,6},{6,4},{5,7},{7,5},{8,10},{10,8},{9,1... | collective-permute-start | bytes 1179656 | tf_op jit(solution)/shard_map/ppermute | solution.py:415
  45.7 22.1 %all-gather.3 = s16[512,3,8,128]{3,2,1,0:T(8,128)(2,1)S(1)} all-gather(s16[64,3,8,128]{3,2,1,0:T(8,128)(2,1)S(1)} %get-tuple-element.9), channel_id=2, replica_groups=mesh['yh'=4,'yl'=2,'x'=4,'zh'=4,'zl'=2,'c'=2] {'x','c'}, dimensions={0}, use_global_device_ids=true | all-gather | bytes 3538944 | tf_op jit(solution)/shard_map/all_gather | solution.py:416
  67.9 0.0 collective-permute-done.far
  67.9 3.5 %shard_map.96 = s16[208,256]{1,0:T(8,128)(2,1)S(1)} custom-call(s32[1]{0:T(128)} %bitcast.17.place, s16[8,4,4,2,2,3,8,128]{7,6,5,4,3,2,1,0:T(8,128)(2,1)S(1)} %bitcast.30, s16[64,3,8,128]{3,2,1,0:T(8,128)(2,1)S(1)} %get-tuple-element.8.near, s16[64,3,8,128]{3,2,1,0:T(8,128)(2,1)S(1)} %collective-permute-done.far), custom_call_target="tpu_custom_call" | custom-call | tf_op jit(solution)/shard_map/pallas_call | solution.py:269
  71.4 0.0 copy-start
  71.4 5.1 %all-gather.1 = s16[416,256]{1,0:T(8,128)(2,1)S(1)} all-gather(s16[208,256]{1,0:T(8,128)(2,1)S(1)} %shard_map.96), channel_id=3, replica_groups=mesh['yh'=4,'yl'=2,'x'=4,'zh'=4,'zl'=2,'c'=2] {'zl'}, dimensions={0}, use_global_device_ids=true | all-gather | bytes 319488 | tf_op jit(solution)/shard_map/all_gather | solution.py:419
  76.5 1.6 %shard_map.97 = bf16[64,24,128]{2,1,0:T(8,128)(2,1)S(1)} custom-call(s16[8,4,4,2,2,3,8,128]{7,6,5,4,3,2,1,0:T(8,128)(2,1)S(1)} %bitcast.31, s16[2,208,256]{2,1,0:T(8,128)(2,1)S(1)} %bitcast.33), custom_call_target="tpu_custom_call" | custom-call | tf_op jit(solution)/shard_map/pallas_call | solution.py:350
  78.1 21.4 %all_to_all.10 = bf16[64,24,128]{2,1,0:T(8,128)(2,1)S(1)} all-to-all(bf16[64,24,128]{2,1,0:T(8,128)(2,1)S(1)} %shard_map.97), channel_id=1, replica_groups=mesh['yh'=4,'yl'=2,'x'=4,'zh'=4,'zl'=2,'c'=2] {'yh','zh','yl','zl'}, dimensions={0} | all-to-all | bytes 786432 | tf_op jit(solution)/shard_map/all_to_all | solution.py:421
  99.5 0.0 copy-done
  99.5 1.1 %shard_map.98 = bf16[4,2048]{1,0:T(4,128)(2,1)} custom-call(bf16[16,2,2,24,128]{4,3,2,1,0:T(8,128)(2,1)S(1)} %bitcast.32, f32[4,128]{1,0:T(4,128)S(1)} %copy-done), custom_call_target="tpu_custom_call" | custom-call | tf_op jit(solution)/shard_map/pallas_call | solution.py:397
Async XLA Ops:
  4.4 39.1 %all-to-all-start = ((s16[64,6,8,128]{3,2,1,0:T(8,128)(2,1)}), s16[64,6,8,128]{3,2,1,0:T(8,128)(2,1)S(1)}, u32[]{:S(2)}, u32[]{:S(2)}) async-start(s16[64,6,8,128]{3,2,1,0:T(8,128)(2,1)} %get-tuple-element.6), calls=%async_computation | async-start | bytes 1572864 | tf_op jit(solution)/shard_map/all_to_all | solution.py:413
  43.6 24.2 %collective-permute-start = (s16[64,3,8,128]{3,2,1,0:T(8,128)(2,1)S(1)}, s16[64,3,8,128]{3,2,1,0:T(8,128)(2,1)S(1)}, u32[]{:S(2)}, u32[]{:S(2)}) collective-permute-start(s16[64,3,8,128]{3,2,1,0:T(8,128)(2,1)S(1)} %get-tuple-element.8.near), channel_id=1, source_target_pairs={{0,2},{2,0},{1,3},{3,1},{4,6},{6,4},{5,7},{7,5},{8,10},{10,8},{9,1... | collective-permute-start | bytes 1179656 | tf_op jit(solution)/shard_map/ppermute | solution.py:415
  71.4 28.1 %copy-start = (f32[4,128]{1,0:T(4,128)S(1)}, f32[4,128]{1,0:T(4,128)}, u32[]{:S(2)}) copy-start(f32[4,128]{1,0:T(4,128)} %get-tuple-element.7.weighted) | copy-start | bytes 6148

commit v7 on v6

--- a/solution.py
+++ b/solution.py
@@ -30,7 +30,7 @@
 ACT_UNIT = ACT_BOUND / LEVELS**7
 
 AXES = ("yh", "yl", "x", "zh", "zl", "c")
-OWNERS = ("yh", "zh", "yl", "zl")
+OWNERS = ("yl", "yh", "zl", "zh")
 COPIES = ("x", "c")
 
 
@@ -107,6 +107,7 @@
         down = []
         for d in range(group):
             owner = i * group + d
+            place = (d % 4 // 2, i // 2, d % 2, i % 2 * 2 + d // 4)
             for m in range(3):
                 value = adam_tile(
                     master[m, owner], moment_one[m, owner], moment_two[m, owner],
@@ -114,21 +115,21 @@
                 )
                 updated[m, owner] = value
                 if m < 2:
-                    codes[owner, m] = encode(value, BOUND).astype(jnp.int16)
+                    codes[(*place, m)] = encode(value, BOUND).astype(jnp.int16)
                 else:
                     down.append(encode(value, BOUND))
             if d % 2:
                 first, second = down[d - 1], down[d]
                 low = jnp.where(pair_rows, first, pltpu.roll(second, 2, 0))
                 high = jnp.where(pair_rows, pltpu.roll(first, 6, 0), second)
-                codes[owner - 1, 2] = low.astype(jnp.int16)
-                codes[owner, 2] = high.astype(jnp.int16)
-            slot = (step * (codes.shape[0] // 4) + i * (group // 4) + d // 4) * CAP
+                codes[(*place[:2], 0, place[3], 2)] = low.astype(jnp.int16)
+                codes[(*place, 2)] = high.astype(jnp.int16)
+            slot = (step * (master.shape[1] // 4) + i * (group // 4) + d // 4) * CAP
             for j in range(CAP):
-                codes[owner, 3 + j] = chosen[slot + j, d % 2]
+                codes[(*place, 3 + j)] = chosen[slot + j, d % 2]
         return carry
 
-    lax.fori_loop(0, codes.shape[0] // group, some, 0)
+    lax.fori_loop(0, master.shape[1] // group, some, 0)
 
 
 def prepare(master, moment_one, moment_two, gradient, states, norm_gain, routes, route_weights, owners):
@@ -142,13 +143,13 @@
         grid=(steps,),
         out_shape=(
             jax.ShapeDtypeStruct(master.shape, jnp.float32),
-            jax.ShapeDtypeStruct((owners, 3 + CAP, 8, 128), jnp.int16),
+            jax.ShapeDtypeStruct((2, 4, 2, 4, 3 + CAP, 8, 128), jnp.int16),
             jax.ShapeDtypeStruct((count, 128), jnp.float32),
         ),
         in_specs=[rows] * 4 + [whole(array) for array in small],
         out_specs=(
             rows,
-            pl.BlockSpec((owners // steps, 3 + CAP, 8, 128), lambda i: (i, 0, 0, 0)),
+            pl.BlockSpec((2, 4 // steps, 2, 4, 3 + CAP, 8, 128), lambda i: (0, i, 0, 0, 0, 0, 0)),
             pl.BlockSpec((count, 128), lambda i: (0, 0)),
         ),
         scratch_shapes=[
@@ -191,14 +192,14 @@
 
 def gate_kernel(place, codes, near, far, out, packed, lines):
     copies = codes.shape[0]
-    xs, yhs, zhs = copies // 2, codes.shape[1], codes.shape[2]
+    xs, yhs, zhs = copies // 2, codes.shape[2], codes.shape[4]
     rows = near.shape[0] * CAP
 
     def extremes(step, carry):
         high, low = carry
         p = step // yhs
         yh = step % yhs
-        block = codes[p, yh].astype(jnp.int32).reshape(zhs * 4, 3, 8, 128)
+        block = codes[p, :, yh].astype(jnp.int32).reshape(zhs * 4, 3, 8, 128)
         return jnp.maximum(high, jnp.max(block, axis=0)), jnp.minimum(low, jnp.min(block, axis=0))
 
     zero = jnp.zeros((3, 8, 128), jnp.int32)
@@ -217,7 +218,8 @@
         factor = factors[m][None]
 
         def values(p, yh, yl):
-            block = codes[p, yh, :, yl, :, m].reshape(zhs * 2, 8, 128)
+            halves = [codes[p, yl, yh, zl, :, m] for zl in range(2)]
+            block = jnp.stack(halves, axis=1).reshape(zhs * 2, 8, 128)
             return level_value(block.astype(jnp.int32).astype(jnp.float32), factor)
 
         def step(t, carry):
@@ -281,7 +283,7 @@
 
 def down_kernel(codes, acts, out, packed, spread):
     copies = codes.shape[0]
-    xs, yhs, zhs = copies // 2, codes.shape[1], codes.shape[2]
+    xs, yhs, zhs = copies // 2, codes.shape[2], codes.shape[4]
     rows = acts.shape[1] - 16
     sub = lax.broadcasted_iota(jnp.int32, (8, 128), 0)
     marks = acts[:, rows : rows + 16].astype(jnp.int32).astype(jnp.float32)
@@ -302,7 +304,7 @@
     low_half = (lax.broadcasted_iota(jnp.int32, (zhs, 8, 128), 1)) < 4
 
     def values(p, yh, yl, zl):
-        block = codes[p, yh, :, yl, zl, 2]
+        block = codes[p, yl, yh, zl, :, 2]
         return level_value(block.astype(jnp.int32).astype(jnp.float32), factor)
 
     def step(i, carry):
@@ -361,7 +363,7 @@
 
 
 def combine_kernel(returned, weighted, out, total):
-    experts, lines = returned.shape[0], returned.shape[3]
+    experts, lines = E, returned.shape[4]
     width = lines // CAP
     rows = weighted.shape[0]
     weights = weighted[...]
@@ -370,8 +372,8 @@
         for j in range(CAP):
             slot = e * CAP + j
             for zl in range(2):
-                value = returned[e, 0, zl, j * width : (j + 1) * width].astype(jnp.float32)
-                value = value + returned[e, 1, zl, j * width : (j + 1) * width].astype(jnp.float32)
+                value = returned[0, e // 4, zl, e % 4, j * width : (j + 1) * width].astype(jnp.float32)
+                value = value + returned[1, e // 4, zl, e % 4, j * width : (j + 1) * width].astype(jnp.float32)
                 for t in range(rows):
                     sums[zl][t] = sums[zl][t] + weights[t : t + 1, slot : slot + 1] * value
     source = lax.broadcasted_iota(jnp.int32, (128, 256), 0)
@@ -392,7 +394,7 @@
 
 def combine(returned, weighted):
     rows = weighted.shape[0]
-    width = returned.shape[3] // CAP
+    width = returned.shape[4] // CAP
     vmem = pl.BlockSpec(memory_space=pltpu.VMEM)
     return pl.pallas_call(
         combine_kernel,
@@ -410,16 +412,17 @@
     updated, codes, weighted = prepare(
         *state, states, norm_gain[None, :], routes, route_weights, owners
     )
+    codes = codes.reshape(owners, 3 + CAP, 8, 128)
     received = lax.all_to_all(codes, OWNERS, split_axis=0, concat_axis=0, tiled=True)
     near = received[:, 3:]
     far = lax.ppermute(near, "zl", [(0, 1), (1, 0)])
     gathered = lax.all_gather(received[:, :3], COPIES, axis=0, tiled=False)
     place = lax.axis_index("zl").astype(jnp.int32).reshape(1)
-    gathered = gathered.reshape(-1, 4, 4, 2, 2, 3, 8, 128)
+    gathered = gathered.reshape(-1, 2, 4, 2, 4, 3, 8, 128)
     acts = lax.all_gather(gate_up(place, gathered, near, far), "zl", axis=0, tiled=False)
     partial_value = down(gathered, acts)
     returned = lax.all_to_all(partial_value, OWNERS, split_axis=0, concat_axis=0, tiled=True)
-    mixture = combine(returned.reshape(E, 2, 2, -1, 128), weighted)
+    mixture = combine(returned.reshape(2, 4, 2, 4, -1, 128), weighted)
     return (from_tiles(updated), mixture)
 
 

time: 102 us -> 102 us (level)
  blocking collectives: 48.6 us -> 47 us
  starting transfers between devices: 19.2 us -> 20.4 us
    all_to_all x1, blocking collectives: 21.4 us -> 19.8 us  [body(): lax.all_to_all(partial_value, OWNERS, split_axis=0, concat_axis=0, tiled=...]
    ppermute x1, starting transfers between devices: 2.11 us -> 3.26 us  [body(): far = lax.ppermute(near, 'zl', [(0, 1), (1, 0)])]
where the time goes in v7:
time: 102 us; the launch traced here: 99.9 us
  blocking collectives  47 us (46%)
  waiting for transfers between devices  21.8 us (21%)
  starting transfers between devices  20.4 us (20%)
  Pallas kernels  9.97 us (10%)
    all_gather x1, blocking collectives, body(): gathered = lax.all_gather(received[:, :3], COPIES, axis=0, tiled=False)  22.1 us
    all_to_all x1, waiting for transfers between devices, body(): lax.all_to_all(codes, OWNERS, split_axis=0, concat_axis=0, tiled=True)  21.8 us
    all_to_all x1, blocking collectives, body(): lax.all_to_all(partial_value, OWNERS, split_axis=0, concat_axis=0, tiled=...  19.8 us
    all_to_all x1, starting transfers between devices, body(): lax.all_to_all(codes, OWNERS, split_axis=0, concat_axis=0, tiled=True)  17.1 us
    all_gather x1, blocking collectives, body(): lax.all_gather(gate_up(place, gathered, near, far), 'zl', axis=0, tiled=F...  5.11 us
    pallas_call x1, Pallas kernels, prepare(): pl.pallas_call(owner_kernel, grid=(steps,), out_shape=(jax.ShapeDtypeStru...  3.79 us
    pallas_call x1, Pallas kernels, gate_up(): pl.pallas_call(gate_kernel, out_shape=jax.ShapeDtypeStruct((sources * CAP...  3.49 us
    ppermute x1, starting transfers between devices, body(): far = lax.ppermute(near, 'zl', [(0, 1), (1, 0)])  3.26 us
  transfers between devices with their start and end apart: 2, of which 1 were waited for; matrix products, arithmetic and copies ran while one was open for 0% of the time, Pallas kernels for 0%

profile of v7, /device:TPU:1, one launch (start us, length us, event | category | flops | bytes accessed | tf_op | source)
XLA Modules:
  0.0 99.9 jit_solution(14280718528458011656)
XLA Ops:
  0.6 3.8 %shard_map.95 = (f32[3,64,8,128]{3,2,1,0:T(8,128)}, s16[2,4,2,4,6,8,128]{6,5,4,3,2,1,0:T(8,128)(2,1)}, f32[4,128]{1,0:T(4,128)}) custom-call(f32[3,64,8,128]{3,2,1,0:T(8,128)} %bitcast.36, f32[3,64,8,128]{3,2,1,0:T(8,128)} %bitcast.37, f32[3,64,8,128]{3,2,1,0:T(8,128)} %bitcast.38, bf16[3,64,8,128]{3,2,1,0:T(8,128)(2,1)} %bitcast.39, ...), custom_call_target="tpu_custom_call" | custom-call | tf_op jit(solution)/shard_map/pallas_call | solution.py:141
  4.4 17.1 %all-to-all-start = ((s16[64,6,8,128]{3,2,1,0:T(8,128)(2,1)}), s16[64,6,8,128]{3,2,1,0:T(8,128)(2,1)S(1)}, u32[]{:S(2)}, u32[]{:S(2)}) async-start(s16[64,6,8,128]{3,2,1,0:T(8,128)(2,1)} %bitcast.35), calls=%async_computation | async-start | bytes 1572864 | tf_op jit(solution)/shard_map/all_to_all | solution.py:416
  21.6 21.8 %all-to-all-done = s16[64,6,8,128]{3,2,1,0:T(8,128)(2,1)S(1)} async-done(((s16[64,6,8,128]{3,2,1,0:T(8,128)(2,1)}), s16[64,6,8,128]{3,2,1,0:T(8,128)(2,1)S(1)}, u32[]{:S(2)}, u32[]{:S(2)}) %all-to-all-start) | async-done | bytes 786464 | tf_op jit(solution)/shard_map/all_to_all | solution.py:416
  43.4 0.1 fusion
  43.4 3.3 %collective-permute-start = (s16[64,3,8,128]{3,2,1,0:T(8,128)(2,1)S(1)}, s16[64,3,8,128]{3,2,1,0:T(8,128)(2,1)S(1)}, u32[]{:S(2)}, u32[]{:S(2)}) collective-permute-start(s16[64,3,8,128]{3,2,1,0:T(8,128)(2,1)S(1)} %get-tuple-element.8.near), channel_id=1, source_target_pairs={{0,2},{2,0},{1,3},{3,1},{4,6},{6,4},{5,7},{7,5},{8,10},{10,8},{9,1... | collective-permute-start | bytes 1179656 | tf_op jit(solution)/shard_map/ppermute | solution.py:418
  46.7 22.1 %all-gather.3 = s16[512,3,8,128]{3,2,1,0:T(8,128)(2,1)S(1)} all-gather(s16[64,3,8,128]{3,2,1,0:T(8,128)(2,1)S(1)} %get-tuple-element.9), channel_id=2, replica_groups=mesh['yh'=4,'yl'=2,'x'=4,'zh'=4,'zl'=2,'c'=2] {'x','c'}, dimensions={0}, use_global_device_ids=true | all-gather | bytes 3538944 | tf_op jit(solution)/shard_map/all_gather | solution.py:419
  68.8 0.0 collective-permute-done.far
  68.8 3.5 %shard_map.96 = s16[208,256]{1,0:T(8,128)(2,1)S(1)} custom-call(s32[1]{0:T(128)} %bitcast.18.place, s16[8,2,4,2,4,3,8,128]{7,6,5,4,3,2,1,0:T(8,128)(2,1)S(1)} %bitcast.31, s16[64,3,8,128]{3,2,1,0:T(8,128)(2,1)S(1)} %get-tuple-element.8.near, s16[64,3,8,128]{3,2,1,0:T(8,128)(2,1)S(1)} %collective-permute-done.far), custom_call_target="tpu_custom_call" | custom-call | tf_op jit(solution)/shard_map/pallas_call | solution.py:271
  72.3 0.0 copy-start
  72.3 5.1 %all-gather.1 = s16[416,256]{1,0:T(8,128)(2,1)S(1)} all-gather(s16[208,256]{1,0:T(8,128)(2,1)S(1)} %shard_map.96), channel_id=3, replica_groups=mesh['yh'=4,'yl'=2,'x'=4,'zh'=4,'zl'=2,'c'=2] {'zl'}, dimensions={0}, use_global_device_ids=true | all-gather | bytes 319488 | tf_op jit(solution)/shard_map/all_gather | solution.py:422
  77.4 1.6 %shard_map.97 = bf16[64,24,128]{2,1,0:T(8,128)(2,1)S(1)} custom-call(s16[8,2,4,2,4,3,8,128]{7,6,5,4,3,2,1,0:T(8,128)(2,1)S(1)} %bitcast.32, s16[2,208,256]{2,1,0:T(8,128)(2,1)S(1)} %bitcast.34), custom_call_target="tpu_custom_call" | custom-call | tf_op jit(solution)/shard_map/pallas_call | solution.py:352
  79.0 19.8 %all_to_all.10 = bf16[64,24,128]{2,1,0:T(8,128)(2,1)S(1)} all-to-all(bf16[64,24,128]{2,1,0:T(8,128)(2,1)S(1)} %shard_map.97), channel_id=1, replica_groups=mesh['yh'=4,'yl'=2,'x'=4,'zh'=4,'zl'=2,'c'=2] {'yl','yh','zl','zh'}, dimensions={0} | all-to-all | bytes 786432 | tf_op jit(solution)/shard_map/all_to_all | solution.py:424
  98.8 0.0 copy-done
  98.8 1.1 %shard_map.98 = bf16[4,2048]{1,0:T(4,128)(2,1)} custom-call(bf16[2,4,2,4,24,128]{5,4,3,2,1,0:T(8,128)(2,1)S(1)} %bitcast.33, f32[4,128]{1,0:T(4,128)S(1)} %copy-done), custom_call_target="tpu_custom_call" | custom-call | tf_op jit(solution)/shard_map/pallas_call | solution.py:399
Async XLA Ops:
  4.4 38.9 %all-to-all-start = ((s16[64,6,8,128]{3,2,1,0:T(8,128)(2,1)}), s16[64,6,8,128]{3,2,1,0:T(8,128)(2,1)S(1)}, u32[]{:S(2)}, u32[]{:S(2)}) async-start(s16[64,6,8,128]{3,2,1,0:T(8,128)(2,1)} %bitcast.35), calls=%async_computation | async-start | bytes 1572864 | tf_op jit(solution)/shard_map/all_to_all | solution.py:416
  43.4 25.3 %collective-permute-start = (s16[64,3,8,128]{3,2,1,0:T(8,128)(2,1)S(1)}, s16[64,3,8,128]{3,2,1,0:T(8,128)(2,1)S(1)}, u32[]{:S(2)}, u32[]{:S(2)}) collective-permute-start(s16[64,3,8,128]{3,2,1,0:T(8,128)(2,1)S(1)} %get-tuple-element.8.near), channel_id=1, source_target_pairs={{0,2},{2,0},{1,3},{3,1},{4,6},{6,4},{5,7},{7,5},{8,10},{10,8},{9,1... | collective-permute-start | bytes 1179656 | tf_op jit(solution)/shard_map/ppermute | solution.py:418
  72.3 26.6 %copy-start = (f32[4,128]{1,0:T(4,128)S(1)}, f32[4,128]{1,0:T(4,128)}, u32[]{:S(2)}) copy-start(f32[4,128]{1,0:T(4,128)} %get-tuple-element.7.weighted) | copy-start | bytes 6148
